TPU v7x, 128 devices: a whole 4x4x4 slice. The times are simulated.
128 devices in a mesh: group: 8 (over z, core), block: 16 (over y, x).
Axes of the slice: x: 4, y: 4, z: 4, core: 2. Of those that a mesh axis runs over, the one named last changes fastest.
Arguments:
- embeddings: float32 [65536, 1024], P(('group', 'block')), may hold values from -6 to 6
- labels: int32 [65536, 1], P(('group', 'block')), may hold values from 0 to 7; in each aligned block of 512 rows (0 to 511, 512 to 1023, ...) at most 96 rows name the same one
- row_ids: int32 [65536], P(('group', 'block')), may hold values from 0 to 65535, each once
Outputs:
- dup_score: float32 [65536], P(('group', 'block'))
Inputs may be any that keep to these rules, and one draw needn't show every extreme that they name: `labels`: among the rows of one device (aligned blocks of 512 rows) no cluster appears more than 96 times; some cluster appears exactly 96 times. `row_ids`: every value appears exactly once.
All inputs are finite; a program needn't handle non-finite values.
Results may differ from a plain program's by a relative error of at most 0.0012.
Values may be sent and summed in bfloat16 or wider, within the bound.
No kernel may reach another device: no remote copies, remote signals or barrier semaphores. Data moves between devices by JAX's collectives and lax.ppermute only.
A program may use at most 128 MiB of HBM per device.

v0:
```python
import functools
import jax
import jax.numpy as jnp
from jax import lax
from jax.experimental import pallas as pl
from jax.experimental.pallas import tpu as pltpu
from jax.sharding import PartitionSpec as P

SIDE = 4
CORES = 2
ROWS = 512
FEATURES = 1024
GROUPS = 8
CAPACITY = 96
EXTRA = 16
SENT = CAPACITY + EXTRA
JOINED = CORES * CAPACITY + EXTRA
BLOCK = GROUPS * CAPACITY
PART = BLOCK // 2
FIRST = PART + EXTRA
MIB = 1 << 20
AXES = ("group", "block")
VMEM = pl.BlockSpec(memory_space=pltpu.VMEM)
NT = (((1,), (1,)), ((), ()))


def column_of(row):
    return jnp.transpose(jnp.broadcast_to(row, (128, row.shape[1])))


def spread(row, lanes):
    return jnp.concatenate([column_of(row)] * (lanes // 128), axis=1)


def prepare_kernel(emb_ref, key_ref, keep_ref, give_ref, place_ref, normed_ref):
    labels = key_ref[...] >> 16
    ids = key_ref[...] & 65535
    group = lax.axis_index("group")
    core, x, z = group & 1, lax.axis_index("block") & (SIDE - 1), group >> 1
    before = lax.broadcasted_iota(jnp.int32, (ROWS, ROWS), 0) < lax.broadcasted_iota(jnp.int32, (ROWS, ROWS), 1)
    alike = spread(labels, ROWS) == labels
    rank = jnp.sum((before & alike).astype(jnp.int32), axis=0, keepdims=True)
    plane = labels & (SIDE - 1)
    other = (labels >> 2) != core
    target = plane * SENT + rank

    def pick(target, count):
        return (lax.broadcasted_iota(jnp.int32, (count, ROWS), 0) == target).astype(jnp.bfloat16)

    slot = plane + jnp.where(other, SIDE, 0)
    place_ref[...] = slot * 128 + rank
    kind = lax.broadcasted_iota(jnp.int32, (8, ROWS), 0)
    digits = jnp.where(kind == 0, ids & 255, jnp.where(kind == 1, ids >> 8, jnp.where(kind == 2, 1, 0)))
    digits = jnp.concatenate([jnp.where(slot == n, digits, 0) for n in range(GROUPS)], axis=0)
    lane = jnp.where(labels < SIDE, z, x) * (CORES * CAPACITY) + jnp.where(other, CAPACITY, 0) + rank
    digits = lax.dot_general(digits.astype(jnp.float32).astype(jnp.bfloat16), pick(lane, FEATURES), NT,
                             preferred_element_type=jnp.float32)
    values = emb_ref[...]
    scale = lax.rsqrt(jnp.sum(values * values, axis=1, keepdims=True) + 1e-06)
    normed_ref[...] = (values * scale).astype(jnp.bfloat16)
    for out_ref, chosen, first in ((give_ref, other, SIDE), (keep_ref, jnp.logical_not(other), 0)):
        moved = jnp.dot(pick(jnp.where(chosen, target, -1), SIDE * SENT), normed_ref[...],
                        preferred_element_type=jnp.float32)
        out_ref[...] = moved.astype(jnp.bfloat16)
        for n in range(SIDE):
            extra = jnp.concatenate(
                [digits[8 * (first + n):8 * (first + n) + 8], jnp.zeros((8, FEATURES), jnp.float32)], axis=0)
            out_ref[n * SENT + CAPACITY:(n + 1) * SENT, :] = extra.astype(jnp.bfloat16)


def prepare(embeddings, keys):
    return pl.pallas_call(
        prepare_kernel,
        out_shape=(
            jax.ShapeDtypeStruct((SIDE * SENT, FEATURES), jnp.bfloat16),
            jax.ShapeDtypeStruct((SIDE * SENT, FEATURES), jnp.bfloat16),
            jax.ShapeDtypeStruct((1, ROWS), jnp.int32),
        ),
        in_specs=[VMEM] * 2,
        out_specs=(VMEM,) * 3,
        scratch_shapes=[pltpu.VMEM((ROWS, FEATURES), jnp.bfloat16)],
        compiler_params=pltpu.CompilerParams(vmem_limit_bytes=32 * MIB),
        name="prepare",
    )(embeddings, keys)


def plane():
    group = lax.axis_index("group")
    return jnp.where((group & 1) == 1, lax.axis_index("block") & (SIDE - 1), group >> 1)


def join_kernel(keep_ref, got_ref, *out_refs):
    for n in range(SIDE):
        start = ((plane() + n) & (SIDE - 1)) * SENT
        extra = jnp.zeros((EXTRA, FEATURES), jnp.float32)
        for i, ref in enumerate((keep_ref, got_ref)):
            rows = ref[pl.ds(pl.multiple_of(start, 16), CAPACITY), :]
            out_refs[n][i * CAPACITY:(i + 1) * CAPACITY, :] = rows
            extra = extra + ref[pl.ds(pl.multiple_of(start + CAPACITY, 16), EXTRA), :].astype(jnp.float32)
        out_refs[n][JOINED - EXTRA:JOINED, :] = extra.astype(jnp.bfloat16)


def join(keep, got):
    return pl.pallas_call(
        join_kernel,
        out_shape=(jax.ShapeDtypeStruct((JOINED, FEATURES), jnp.bfloat16),) * SIDE,
        in_specs=[VMEM] * 2, out_specs=(VMEM,) * SIDE,
        compiler_params=pltpu.CompilerParams(vmem_limit_bytes=16 * MIB),
        name="join",
    )(keep, got)


def gather_kernel(*refs):
    out_ref = refs[SIDE]
    extra = jnp.zeros((EXTRA, FEATURES), jnp.float32)
    size = CORES * CAPACITY
    for n in range(SIDE):
        source = (plane() - n) & (SIDE - 1)
        start = source * size + (source >> 1) * EXTRA
        out_ref[pl.ds(pl.multiple_of(start, 16), size), :] = refs[n][0:size, :]
        extra = extra + refs[n][size:JOINED, :].astype(jnp.float32)
    out_ref[PART:FIRST, :] = extra.astype(jnp.bfloat16)


def gather(pieces):
    return pl.pallas_call(
        gather_kernel,
        out_shape=jax.ShapeDtypeStruct((BLOCK + EXTRA, FEATURES), jnp.bfloat16),
        in_specs=[VMEM] * SIDE, out_specs=VMEM,
        compiler_params=pltpu.CompilerParams(vmem_limit_bytes=16 * MIB),
        name="gather",
    )(*pieces)


def column_keys(extra):
    digits = extra[:, 0:BLOCK].astype(jnp.float32)
    return digits[0:1] + digits[1:2] * 256.0 + (1.0 - digits[2:3]) * 131072.0


def row_keys(extra):
    digit = lax.broadcasted_iota(jnp.int32, (EXTRA, 128), 0)
    weight = jnp.where(digit == 0, 1.0, jnp.where(digit == 1, 256.0, jnp.where(digit == 2, -131072.0, 0.0)))
    keys = lax.dot_general(extra[:, 0:BLOCK], weight.astype(jnp.bfloat16), (((0,), (0,)), ((), ())),
                           preferred_element_type=jnp.float32)
    return keys + 131072.0


def lane_tiles(values):
    return functools.reduce(jnp.maximum, [values[:, n:n + 128] for n in range(0, BLOCK, 128)])


def halves(refs):
    if len(refs) == 1:
        return refs[0].at[0:PART], refs[0].at[FIRST:FIRST + PART]
    return refs[0].at[0:PART], refs[1]


def scores_of(left, right):
    return lax.dot_general(left, right, NT, preferred_element_type=jnp.float32)


class Whole:
    def __init__(self, wanted, held, sems):
        self.copies = []
        for i, refs in enumerate(wanted):
            for n, part in enumerate(halves(refs)):
                self.copies.append(
                    pltpu.make_async_copy(part, held.at[i, n * PART:(n + 1) * PART], sems.at[2 * i + n]))
        for copy in self.copies:
            copy.start()

    def wait(self, i):
        self.copies[2 * i].wait()
        self.copies[2 * i + 1].wait()


NAMES = ("own", "up", "um", "uo", "yp", "yo")


def by_group(row):
    empty = jnp.zeros((1, 128 - CAPACITY), jnp.float32)
    return jnp.concatenate(
        [jnp.concatenate([row[:, n * CAPACITY:(n + 1) * CAPACITY], empty], axis=1) for n in range(GROUPS)], axis=0)


def compare_kernel(sizes, products, ready, before_ref, *refs):
    sources = {}
    for block, size in sizes:
        sources[block], refs = refs[:size], refs[size:]
    out_refs, (held, sems) = refs[:-2], refs[-2:]
    whole = Whole([sources[columns] for columns, _ in products], held, sems)
    extras = {block: refs_of[0][PART:FIRST, :] for block, refs_of in sources.items()}
    found = {}

    def note(name, values):
        found[name] = jnp.maximum(found[name], values) if name in found else values

    for i, (columns, uses) in enumerate(products):
        theirs = column_keys(extras[columns])
        columns_best = jnp.full((8, BLOCK), -1.0, jnp.float32)
        whole.wait(i)
        for rows, for_rows, for_columns in uses:
            keys = row_keys(extras[rows])
            rows_best = []
            for part, r in zip(halves(sources[rows]), (0, PART)):
                own = jnp.concatenate([keys[r:r + PART, :]] * (BLOCK // 128), axis=1)
                scores = scores_of(part[...], held[i])
                earlier = theirs < own
                if for_rows:
                    rows_best.append(lane_tiles(jnp.where(earlier, scores, -1.0)))
                if for_columns:
                    later = jnp.where(earlier, -1.0, scores)
                    columns_best = jnp.maximum(columns_best, jnp.max(later.reshape(PART // 8, 8, BLOCK), axis=0))
            if for_rows:
                note(rows, jnp.max(jnp.transpose(jnp.concatenate(rows_best, axis=0)), axis=0, keepdims=True))
        if any(use[2] for use in uses):
            note(columns, jnp.max(columns_best, axis=0, keepdims=True))
    for n, name in enumerate(NAMES):
        values = before_ref[n:n + 1, :]
        if name in found:
            values = jnp.maximum(values, found[name])
        if name in ready:
            out_refs[1 + ready.index(name)][...] = by_group(values)
        out_refs[0][n:n + 1, :] = values


def compare(blocks, before, products, name, ready=()):
    names = []
    for columns, uses in products:
        for block in [columns] + [use[0] for use in uses]:
            if block not in names:
                names.append(block)
    units = sum(len(uses) for _, uses in products)
    shape = jax.ShapeDtypeStruct((GROUPS, 128), jnp.float32)
    return pl.pallas_call(
        functools.partial(compare_kernel, [(block, len(blocks[block])) for block in names], products, ready),
        out_shape=(jax.ShapeDtypeStruct((8, BLOCK), jnp.float32),) + (shape,) * len(ready),
        in_specs=[VMEM] * (1 + sum(len(blocks[block]) for block in names)),
        out_specs=(VMEM,) * (1 + len(ready)),
        scratch_shapes=[
            pltpu.VMEM((len(products), BLOCK, FEATURES), jnp.bfloat16),
            pltpu.SemaphoreType.DMA((2 * len(products),)),
        ],
        compiler_params=pltpu.CompilerParams(vmem_limit_bytes=36 * MIB),
        cost_estimate=pl.CostEstimate(flops=2 * units * BLOCK * BLOCK * FEATURES,
                                      bytes_accessed=2 * BLOCK * FEATURES, transcendentals=0),
        name=name,
    )(before, *[part for block in names for part in blocks[block]])


def finish_kernel(place_ref, kept_ref, got_ref, out_ref):
    rows = [kept_ref[CORES * n:CORES * n + 1, :] for n in range(SIDE)]
    rows = rows + [got_ref[CORES * n + 1:CORES * n + 2, :] for n in range(SIDE)]
    columns = jnp.transpose(jnp.concatenate(rows + [jnp.zeros((128 - GROUPS, 128), jnp.float32)], axis=0))
    best = jnp.full((128, ROWS), -2.0, jnp.float32)
    here = lax.broadcasted_iota(jnp.int32, (128, ROWS), 0)
    for n in range(GROUPS):
        best = jnp.where(here == place_ref[...] - 128 * n, columns[:, n:n + 1], best)
    out_ref[...] = jnp.max(best, axis=0, keepdims=True)


def device_at(x, y, z, core):
    return (z * CORES + core) * SIDE * SIDE + y * SIDE + x


def everywhere():
    return [(x, y, z, core) for z in range(SIDE) for core in range(CORES) for y in range(SIDE) for x in range(SIDE)]


def move(value, along, up):
    pairs = []
    for x, y, z, core in everywhere():
        dx, dy, dz = (0, -up, along) if core else (along, up, 0)
        pairs.append((device_at(x, y, z, core), device_at((x + dx) % SIDE, (y + dy) % SIDE, (z + dz) % SIDE, core)))
    return lax.ppermute(value, AXES, pairs)


def swap(value):
    pairs = [(device_at(x, y, z, core), device_at(x, y, z, 1 - core)) for x, y, z, core in everywhere()]
    return lax.ppermute(value, AXES, pairs)


def climb(value, planes):
    pairs = []
    for x, y, z, core in everywhere():
        dx, dz = (planes, 0) if core else (0, planes)
        pairs.append((device_at(x, y, z, core), device_at((x + dx) % SIDE, y, (z + dz) % SIDE, core)))
    return lax.ppermute(value, AXES, pairs)


def exchange(value):
    span = range(SIDE)
    lines = [[device_at(x, y, z, 0) for z in span] for x in span for y in span]
    lines = lines + [[device_at(x, y, z, 1) for x in span] for z in span for y in span]
    return lax.all_to_all(value, AXES, split_axis=0, concat_axis=0, tiled=True, axis_index_groups=lines)


def per_device(embeddings, labels, row_ids):
    keys = labels.reshape(ROWS) * 65536 + row_ids
    keep, give, place = prepare(embeddings, keys.reshape(1, ROWS))
    pieces = join(keep, swap(give))
    own = gather([climb(piece, n) if n else piece for n, piece in enumerate(pieces)])
    yp, up, um = move(own, 0, -1), move(own, -1, 0), move(own, 1, 0)
    best = jnp.full((8, BLOCK), -1.0, jnp.float32)
    best, = compare(dict(own=(own,)), best, (("own", (("own", True, False),)),), "compare_own")
    yp, best = lax.optimization_barrier((yp, best))
    yo = move(yp, 0, -1)
    uo = move(up[0:FIRST], -1, 0), move(um[FIRST:FIRST + PART], 1, 0)
    blocks = dict(own=(own,), up=(up,), um=(um,), uo=uo, yp=(yp,), yo=(yo,))
    best, for_um = compare(blocks, best, (
        ("own", (("up", True, True),)),
        ("yp", (("own", True, True), ("up", True, True), ("um", True, True))),
    ), "compare_near", ("um",))
    for_um, best = lax.optimization_barrier((move(for_um, -1, 0), best))
    best, for_uo, for_yp = compare(blocks, best, (
        ("own", (("uo", False, True),)),
        ("yp", (("uo", True, True),)),
    ), "compare_line", ("uo", "yp"))
    back = [for_um, move(for_uo, 2, 0), move(for_yp, 0, 1)]
    best, found, for_up, for_yo = compare(blocks, best, (
        ("yo", (("own", True, False), ("up", True, True), ("uo", False, True))),
    ), "compare_far", ("own", "up", "yo"))
    for_up, for_yo, *back = lax.optimization_barrier((for_up, for_yo, *back))
    back = back + [move(for_up, 1, 0), move(for_yo, 0, 2)]
    found = functools.reduce(jnp.maximum, back, found)
    kept = exchange(found)
    out = pl.pallas_call(
        finish_kernel, out_shape=jax.ShapeDtypeStruct((1, ROWS), jnp.float32), name="finish",
        in_specs=[VMEM] * 3, out_specs=VMEM,
        compiler_params=pltpu.CompilerParams(vmem_limit_bytes=8 * MIB),
    )(place, kept, swap(kept))
    return out.reshape(ROWS)


def solution(mesh):
    placed = (P(AXES, None), P(AXES, None), P(AXES))
    return jax.shard_map(
        per_device, mesh=mesh, in_specs=placed, out_specs=P(AXES), check_vma=False
    )
```

profile of v0, /device:TPU:1, one launch (start us, length us, event | category | flops | bytes accessed | tf_op | source)
XLA Modules:
  0.0 93.4 jit_solution(2985927811386697616)
XLA Ops:
  1.4 1.6 %copy-done = f32[512,1024]{1,0:T(8,128)S(1)} copy-done((f32[512,1024]{1,0:T(8,128)S(1)}, f32[512,1024]{1,0:T(8,128)}, u32[]{:S(2)}) %copy-start) | copy-done | bytes 2097176
  3.0 1.7 %prepare.1 = (bf16[448,1024]{1,0:T(8,128)(2,1)S(1)}, bf16[448,1024]{1,0:T(8,128)(2,1)S(1)}, s32[1,512]{1,0:T(1,128)S(1)}) custom-call(f32[512,1024]{1,0:T(8,128)S(1)} %copy-done, s32[1,512]{1,0:T(1,128)S(1)} %bitcast.7), custom_call_target="tpu_custom_call" | custom-call | tf_op jit(solution)/shard_map/prepare/pallas_call | solution.py:72
  4.7 1.5 %collective-permute-start = (bf16[448,1024]{1,0:T(8,128)(2,1)S(1)}, bf16[448,1024]{1,0:T(8,128)(2,1)S(1)}, u32[]{:S(2)}, u32[]{:S(2)}) collective-permute-start(bf16[448,1024]{1,0:T(8,128)(2,1)S(1)} %get-tuple-element.31), channel_id=1, source_target_pairs={{0,16},{1,17},{2,18},{3,19},{4,20},{5,21},{6,22},{7,23},{8,24},{9,... | collective-permute-start | bytes 2752520 | tf_op jit(solution)/shard_map/ppermute | solution.py:280
  6.2 2.1 %collective-permute-done.got_ref = bf16[448,1024]{1,0:T(8,128)(2,1)S(1)} collective-permute-done((bf16[448,1024]{1,0:T(8,128)(2,1)S(1)}, bf16[448,1024]{1,0:T(8,128)(2,1)S(1)}, u32[]{:S(2)}, u32[]{:S(2)}) %collective-permute-start) | collective-permute-done | bytes 917536 | tf_op jit(solution)/shard_map/ppermute | solution.py:280
  8.4 1.4 %collective-permute-start.1 = (bf16[208,1024]{1,0:T(8,128)(2,1)S(1)}, bf16[208,1024]{1,0:T(8,128)(2,1)S(1)}, u32[]{:S(2)}, u32[]{:S(2)}) collective-permute-start(bf16[208,1024]{1,0:T(8,128)(2,1)S(1)} %get-tuple-element.33), channel_id=1, source_target_pairs={{0,32},{1,33},{2,34},{3,35},{4,36},{5,37},{6,38},{7,39},{8,40},{9,... | collective-permute-start | bytes 1277960 | tf_op jit(solution)/shard_map/ppermute | solution.py:288
  9.8 2.5 %collective-permute-start.2 = (bf16[208,1024]{1,0:T(8,128)(2,1)S(1)}, bf16[208,1024]{1,0:T(8,128)(2,1)S(1)}, u32[]{:S(2)}, u32[]{:S(2)}) collective-permute-start(bf16[208,1024]{1,0:T(8,128)(2,1)S(1)} %get-tuple-element.34), channel_id=1, source_target_pairs={{0,64},{1,65},{2,66},{3,67},{4,68},{5,69},{6,70},{7,71},{8,72},{9,... | collective-permute-start | bytes 1277960 | tf_op jit(solution)/shard_map/ppermute | solution.py:288
  13.4 3.6 %collective-permute-done.1.refs_1_ = bf16[208,1024]{1,0:T(8,128)(2,1)S(1)} collective-permute-done((bf16[208,1024]{1,0:T(8,128)(2,1)S(1)}, bf16[208,1024]{1,0:T(8,128)(2,1)S(1)}, u32[]{:S(2)}, u32[]{:S(2)}) %collective-permute-start.1) | collective-permute-done | bytes 426016 | tf_op jit(solution)/shard_map/ppermute | solution.py:288
  16.9 5.6 %collective-permute-done.2.refs_2_ = bf16[208,1024]{1,0:T(8,128)(2,1)S(1)} collective-permute-done((bf16[208,1024]{1,0:T(8,128)(2,1)S(1)}, bf16[208,1024]{1,0:T(8,128)(2,1)S(1)}, u32[]{:S(2)}, u32[]{:S(2)}) %collective-permute-start.2) | collective-permute-done | bytes 426016 | tf_op jit(solution)/shard_map/ppermute | solution.py:288
  22.7 1.4 %collective-permute-start.4 = (bf16[784,1024]{1,0:T(8,128)(2,1)S(1)}, bf16[784,1024]{1,0:T(8,128)(2,1)S(1)}, u32[]{:S(2)}, u32[]{:S(2)}) collective-permute-start(bf16[784,1024]{1,0:T(8,128)(2,1)S(1)} %gather.1.refs_0_.refs_1_), channel_id=1, source_target_pairs={{0,12},{1,13},{2,14},{3,15},{4,0},{5,1},{6,2},{7,3},{8,4},{9,5},{1... | collective-permute-start | bytes 4816904 | tf_op jit(solution)/shard_map/ppermute | solution.py:275
  24.1 3.5 %collective-permute-start.5 = (bf16[784,1024]{1,0:T(8,128)(2,1)S(1)}, bf16[784,1024]{1,0:T(8,128)(2,1)S(1)}, u32[]{:S(2)}, u32[]{:S(2)}) collective-permute-start(bf16[784,1024]{1,0:T(8,128)(2,1)S(1)} %gather.1.refs_0_.refs_1_), channel_id=1, source_target_pairs={{0,3},{1,0},{2,1},{3,2},{4,7},{5,4},{6,5},{7,6},{8,11},{9,8},{10,9... | collective-permute-start | bytes 4816904 | tf_op jit(solution)/shard_map/ppermute | solution.py:275
  27.5 1.8 %compare_own.1.before_ref = f32[8,768]{1,0:T(8,128)S(1)} custom-call(f32[8,768]{1,0:T(8,128)S(1)} %broadcast_in_dim.3.before_ref, bf16[784,1024]{1,0:T(8,128)(2,1)S(1)} %gather.1.refs_0_.refs_1_), custom_call_target="tpu_custom_call" | custom-call | flops 1207959552 | bytes 1572864 | tf_op jit(solution)/shard_map/compare_own/pallas_call | solution.py:235
  29.3 14.7 %collective-permute-done.4.refs_2_.refs_3_ = bf16[784,1024]{1,0:T(8,128)(2,1)S(1)} collective-permute-done((bf16[784,1024]{1,0:T(8,128)(2,1)S(1)}, bf16[784,1024]{1,0:T(8,128)(2,1)S(1)}, u32[]{:S(2)}, u32[]{:S(2)}) %collective-permute-start.4) | collective-permute-done | bytes 1605664 | tf_op jit(solution)/shard_map/ppermute | solution.py:275
  45.3 3.5 %collective-permute-start.8 = (bf16[400,1024]{1,0:T(8,128)(2,1)S(1)}, bf16[400,1024]{1,0:T(8,128)(2,1)S(1)}, u32[]{:S(2)}, u32[]{:S(2)}) collective-permute-start(bf16[400,1024]{1,0:T(8,128)(2,1)S(1)} %slice.8), channel_id=1, source_target_pairs={{0,3},{1,0},{2,1},{3,2},{4,7},{5,4},{6,5},{7,6},{8,11},{9,8},{10,9... | collective-permute-start | bytes 2457608 | tf_op jit(solution)/shard_map/ppermute | solution.py:275
  48.9 6.3 %compare_near.1 = (f32[8,768]{1,0:T(8,128)S(1)}, f32[8,128]{1,0:T(8,128)S(1)}) custom-call(f32[8,768]{1,0:T(8,128)S(1)} %compare_own.1.before_ref, bf16[784,1024]{1,0:T(8,128)(2,1)S(1)} %gather.1.refs_0_.refs_1_, bf16[784,1024]{1,0:T(8,128)(2,1)S(1)} %collective-permute-done.5.refs_1_.refs_2_, bf16[784,1024]{1,0:T(8,128)(2,1)S(1)} %collective-permute-done.4.refs_2_.refs_3_, ...), custom_call_target="tpu_custom_call" | custom-call | flops 4831838208 | bytes 1572864 | tf_op jit(solution)/shard_map/compare_near/pallas_call | solution.py:235
  55.3 2.9 %collective-permute-start.7 = (f32[8,128]{1,0:T(8,128)S(1)}, f32[8,128]{1,0:T(8,128)S(1)}, u32[]{:S(2)}, u32[]{:S(2)}) collective-permute-start(f32[8,128]{1,0:T(8,128)S(1)} %get-tuple-element.38), channel_id=1, source_target_pairs={{0,3},{1,0},{2,1},{3,2},{4,7},{5,4},{6,5},{7,6},{8,11},{9,8},{10,9... | collective-permute-start | bytes 12296 | tf_op jit(solution)/shard_map/ppermute | solution.py:275
  59.0 2.3 %collective-permute-done.9.refs_2_.refs_4_ = bf16[384,1024]{1,0:T(8,128)(2,1)S(1)} collective-permute-done((bf16[384,1024]{1,0:T(8,128)(2,1)S(1)}, bf16[384,1024]{1,0:T(8,128)(2,1)S(1)}, u32[]{:S(2)}, u32[]{:S(2)}) %collective-permute-start.9) | collective-permute-done | bytes 786464 | tf_op jit(solution)/shard_map/ppermute | solution.py:275
  61.3 3.6 %compare_line.1 = (f32[8,768]{1,0:T(8,128)S(1)}, f32[8,128]{1,0:T(8,128)S(1)}, f32[8,128]{1,0:T(8,128)S(1)}) custom-call(f32[8,768]{1,0:T(8,128)S(1)} %get-tuple-element.40.before_ref, bf16[784,1024]{1,0:T(8,128)(2,1)S(1)} %gather.1.refs_0_.refs_1_, bf16[400,1024]{1,0:T(8,128)(2,1)S(1)} %collective-permute-done.8.refs_1_.refs_3_, ...), custom_call_target="tpu_custom_call" | custom-call | flops 2415919104 | bytes 1572864 | tf_op jit(solution)/shard_map/compare_line/pallas_call | solution.py:235
  64.9 1.6 %collective-permute-start.12 = (f32[8,128]{1,0:T(8,128)S(1)}, f32[8,128]{1,0:T(8,128)S(1)}, u32[]{:S(2)}, u32[]{:S(2)}) collective-permute-start(f32[8,128]{1,0:T(8,128)S(1)} %get-tuple-element.47), channel_id=1, source_target_pairs={{0,4},{1,5},{2,6},{3,7},{4,8},{5,9},{6,10},{7,11},{8,12},{9,13},{1... | collective-permute-start | bytes 12296 | tf_op jit(solution)/shard_map/ppermute | solution.py:275
  66.5 4.9 %compare_far.1 = (f32[8,768]{1,0:T(8,128)}, f32[8,128]{1,0:T(8,128)S(1)}, f32[8,128]{1,0:T(8,128)S(1)}, f32[8,128]{1,0:T(8,128)S(1)}) custom-call(f32[8,768]{1,0:T(8,128)S(1)} %get-tuple-element.41.before_ref, bf16[784,1024]{1,0:T(8,128)(2,1)S(1)} %collective-permute-done.10.refs_0_, bf16[784,1024]{1,0:T(8,128)(2,1)S(1)} %gather.1.refs_0_.refs_1_, ...), custom_call_target="tpu_custom_call" | custom-call | flops 3623878656 | bytes 1572864 | tf_op jit(solution)/shard_map/compare_far/pallas_call | solution.py:235
  71.4 1.5 %collective-permute-start.13 = (f32[8,128]{1,0:T(8,128)S(1)}, f32[8,128]{1,0:T(8,128)S(1)}, u32[]{:S(2)}, u32[]{:S(2)}) collective-permute-start(f32[8,128]{1,0:T(8,128)S(1)} %get-tuple-element.51), channel_id=1, source_target_pairs={{0,1},{1,2},{2,3},{3,0},{4,5},{5,6},{6,7},{7,4},{8,9},{9,10},{10,1... | collective-permute-start | bytes 12296 | tf_op jit(solution)/shard_map/ppermute | solution.py:275
  72.9 1.6 %collective-permute-start.14 = (f32[8,128]{1,0:T(8,128)S(1)}, f32[8,128]{1,0:T(8,128)S(1)}, u32[]{:S(2)}, u32[]{:S(2)}) collective-permute-start(f32[8,128]{1,0:T(8,128)S(1)} %get-tuple-element.52), channel_id=1, source_target_pairs={{0,8},{1,9},{2,10},{3,11},{4,12},{5,13},{6,14},{7,15},{8,0},{9,1},... | collective-permute-start | bytes 12296 | tf_op jit(solution)/shard_map/ppermute | solution.py:275
  75.2 1.7 %collective-permute-done.14 = f32[8,128]{1,0:T(8,128)S(1)} collective-permute-done((f32[8,128]{1,0:T(8,128)S(1)}, f32[8,128]{1,0:T(8,128)S(1)}, u32[]{:S(2)}, u32[]{:S(2)}) %collective-permute-start.14) | collective-permute-done | bytes 4128 | tf_op jit(solution)/shard_map/ppermute | solution.py:275
  76.9 7.9 %all_to_all.11 = f32[4,2,128]{2,1,0:T(2,128)S(1)} all-to-all(f32[4,2,128]{2,1,0:T(2,128)S(1)} %bitcast.8), channel_id=1, replica_groups={{0,32,64,96},{4,36,68,100},{8,40,72,104},{12,44,76,108},{1,33,65,97},{5..., dimensions={0} | all-to-all | bytes 8192 | tf_op jit(solution)/shard_map/all_to_all | solution.py:295
  84.7 6.7 %collective-permute-start.15 = (f32[8,128]{1,0:T(8,128)S(1)}, f32[8,128]{1,0:T(8,128)S(1)}, u32[]{:S(2)}, u32[]{:S(2)}) collective-permute-start(f32[8,128]{1,0:T(8,128)S(1)} %bitcast.5), channel_id=1, source_target_pairs={{0,16},{1,17},{2,18},{3,19},{4,20},{5,21},{6,22},{7,23},{8,24},{9,... | collective-permute-start | bytes 12296 | tf_op jit(solution)/shard_map/ppermute | solution.py:280
  (25 shorter events, 7.7 us)
Async XLA Ops:
  1.4 1.6 %copy-start = (f32[512,1024]{1,0:T(8,128)S(1)}, f32[512,1024]{1,0:T(8,128)}, u32[]{:S(2)}) copy-start(f32[512,1024]{1,0:T(8,128)} %emb_ref.1) | copy-start | bytes 6291460
  4.7 3.6 %collective-permute-start = (bf16[448,1024]{1,0:T(8,128)(2,1)S(1)}, bf16[448,1024]{1,0:T(8,128)(2,1)S(1)}, u32[]{:S(2)}, u32[]{:S(2)}) collective-permute-start(bf16[448,1024]{1,0:T(8,128)(2,1)S(1)} %get-tuple-element.31), channel_id=1, source_target_pairs={{0,16},{1,17},{2,18},{3,19},{4,20},{5,21},{6,22},{7,23},{8,24},{9,... | collective-permute-start | bytes 2752520 | tf_op jit(solution)/shard_map/ppermute | solution.py:280
  8.4 8.6 %collective-permute-start.1 = (bf16[208,1024]{1,0:T(8,128)(2,1)S(1)}, bf16[208,1024]{1,0:T(8,128)(2,1)S(1)}, u32[]{:S(2)}, u32[]{:S(2)}) collective-permute-start(bf16[208,1024]{1,0:T(8,128)(2,1)S(1)} %get-tuple-element.33), channel_id=1, source_target_pairs={{0,32},{1,33},{2,34},{3,35},{4,36},{5,37},{6,38},{7,39},{8,40},{9,... | collective-permute-start | bytes 1277960 | tf_op jit(solution)/shard_map/ppermute | solution.py:288
  9.8 12.8 %collective-permute-start.2 = (bf16[208,1024]{1,0:T(8,128)(2,1)S(1)}, bf16[208,1024]{1,0:T(8,128)(2,1)S(1)}, u32[]{:S(2)}, u32[]{:S(2)}) collective-permute-start(bf16[208,1024]{1,0:T(8,128)(2,1)S(1)} %get-tuple-element.34), channel_id=1, source_target_pairs={{0,64},{1,65},{2,66},{3,67},{4,68},{5,69},{6,70},{7,71},{8,72},{9,... | collective-permute-start | bytes 1277960 | tf_op jit(solution)/shard_map/ppermute | solution.py:288
  12.2 10.4 %collective-permute-start.3 = (bf16[208,1024]{1,0:T(8,128)(2,1)S(1)}, bf16[208,1024]{1,0:T(8,128)(2,1)S(1)}, u32[]{:S(2)}, u32[]{:S(2)}) collective-permute-start(bf16[208,1024]{1,0:T(8,128)(2,1)S(1)} %get-tuple-element.35), channel_id=1, source_target_pairs={{0,96},{1,97},{2,98},{3,99},{4,100},{5,101},{6,102},{7,103},{8,104... | collective-permute-start | bytes 1277960 | tf_op jit(solution)/shard_map/ppermute | solution.py:288
  22.7 21.3 %collective-permute-start.4 = (bf16[784,1024]{1,0:T(8,128)(2,1)S(1)}, bf16[784,1024]{1,0:T(8,128)(2,1)S(1)}, u32[]{:S(2)}, u32[]{:S(2)}) collective-permute-start(bf16[784,1024]{1,0:T(8,128)(2,1)S(1)} %gather.1.refs_0_.refs_1_), channel_id=1, source_target_pairs={{0,12},{1,13},{2,14},{3,15},{4,0},{5,1},{6,2},{7,3},{8,4},{9,5},{1... | collective-permute-start | bytes 4816904 | tf_op jit(solution)/shard_map/ppermute | solution.py:275
  24.1 21.2 %collective-permute-start.5 = (bf16[784,1024]{1,0:T(8,128)(2,1)S(1)}, bf16[784,1024]{1,0:T(8,128)(2,1)S(1)}, u32[]{:S(2)}, u32[]{:S(2)}) collective-permute-start(bf16[784,1024]{1,0:T(8,128)(2,1)S(1)} %gather.1.refs_0_.refs_1_), channel_id=1, source_target_pairs={{0,3},{1,0},{2,1},{3,2},{4,7},{5,4},{6,5},{7,6},{8,11},{9,8},{10,9... | collective-permute-start | bytes 4816904 | tf_op jit(solution)/shard_map/ppermute | solution.py:275
  27.5 21.3 %collective-permute-start.6 = (bf16[784,1024]{1,0:T(8,128)(2,1)S(1)}, bf16[784,1024]{1,0:T(8,128)(2,1)S(1)}, u32[]{:S(2)}, u32[]{:S(2)}) collective-permute-start(bf16[784,1024]{1,0:T(8,128)(2,1)S(1)} %gather.1.refs_0_.refs_1_), channel_id=1, source_target_pairs={{0,1},{1,2},{2,3},{3,0},{4,5},{5,6},{6,7},{7,4},{8,9},{9,10},{10,1... | collective-permute-start | bytes 4816904 | tf_op jit(solution)/shard_map/ppermute | solution.py:275
  44.0 22.5 %collective-permute-start.10 = (bf16[784,1024]{1,0:T(8,128)(2,1)S(1)}, bf16[784,1024]{1,0:T(8,128)(2,1)S(1)}, u32[]{:S(2)}, u32[]{:S(2)}) collective-permute-start(bf16[784,1024]{1,0:T(8,128)(2,1)S(1)} %collective-permute-done.4.refs_2_.refs_3_), channel_id=1, source_target_pairs={{0,12},{1,13},{2,14},{3,15},{4,0},{5,1},{6,2},{7,3},{8,4},{9,5},{1... | collective-permute-start | bytes 4816904 | tf_op jit(solution)/shard_map/ppermute | solution.py:275
  45.3 16.0 %collective-permute-start.8 = (bf16[400,1024]{1,0:T(8,128)(2,1)S(1)}, bf16[400,1024]{1,0:T(8,128)(2,1)S(1)}, u32[]{:S(2)}, u32[]{:S(2)}) collective-permute-start(bf16[400,1024]{1,0:T(8,128)(2,1)S(1)} %slice.8), channel_id=1, source_target_pairs={{0,3},{1,0},{2,1},{3,2},{4,7},{5,4},{6,5},{7,6},{8,11},{9,8},{10,9... | collective-permute-start | bytes 2457608 | tf_op jit(solution)/shard_map/ppermute | solution.py:275
  48.8 12.4 %collective-permute-start.9 = (bf16[384,1024]{1,0:T(8,128)(2,1)S(1)}, bf16[384,1024]{1,0:T(8,128)(2,1)S(1)}, u32[]{:S(2)}, u32[]{:S(2)}) collective-permute-start(bf16[384,1024]{1,0:T(8,128)(2,1)S(1)} %slice.9), channel_id=1, source_target_pairs={{0,1},{1,2},{2,3},{3,0},{4,5},{5,6},{6,7},{7,4},{8,9},{9,10},{10,1... | collective-permute-start | bytes 2359304 | tf_op jit(solution)/shard_map/ppermute | solution.py:275
  55.3 3.7 %collective-permute-start.7 = (f32[8,128]{1,0:T(8,128)S(1)}, f32[8,128]{1,0:T(8,128)S(1)}, u32[]{:S(2)}, u32[]{:S(2)}) collective-permute-start(f32[8,128]{1,0:T(8,128)S(1)} %get-tuple-element.38), channel_id=1, source_target_pairs={{0,3},{1,0},{2,1},{3,2},{4,7},{5,4},{6,5},{7,6},{8,11},{9,8},{10,9... | collective-permute-start | bytes 12296 | tf_op jit(solution)/shard_map/ppermute | solution.py:275
  64.8 6.6 %collective-permute-start.11 = (f32[8,128]{1,0:T(8,128)S(1)}, f32[8,128]{1,0:T(8,128)S(1)}, u32[]{:S(2)}, u32[]{:S(2)}) collective-permute-start(f32[8,128]{1,0:T(8,128)S(1)} %get-tuple-element.46), channel_id=1, source_target_pairs={{0,2},{1,3},{2,0},{3,1},{4,6},{5,7},{6,4},{7,5},{8,10},{9,11},{10,... | collective-permute-start | bytes 12296 | tf_op jit(solution)/shard_map/ppermute | solution.py:275
  64.9 6.5 %collective-permute-start.12 = (f32[8,128]{1,0:T(8,128)S(1)}, f32[8,128]{1,0:T(8,128)S(1)}, u32[]{:S(2)}, u32[]{:S(2)}) collective-permute-start(f32[8,128]{1,0:T(8,128)S(1)} %get-tuple-element.47), channel_id=1, source_target_pairs={{0,4},{1,5},{2,6},{3,7},{4,8},{5,9},{6,10},{7,11},{8,12},{9,13},{1... | collective-permute-start | bytes 12296 | tf_op jit(solution)/shard_map/ppermute | solution.py:275
  71.4 3.7 %collective-permute-start.13 = (f32[8,128]{1,0:T(8,128)S(1)}, f32[8,128]{1,0:T(8,128)S(1)}, u32[]{:S(2)}, u32[]{:S(2)}) collective-permute-start(f32[8,128]{1,0:T(8,128)S(1)} %get-tuple-element.51), channel_id=1, source_target_pairs={{0,1},{1,2},{2,3},{3,0},{4,5},{5,6},{6,7},{7,4},{8,9},{9,10},{10,1... | collective-permute-start | bytes 12296 | tf_op jit(solution)/shard_map/ppermute | solution.py:275
  72.9 4.0 %collective-permute-start.14 = (f32[8,128]{1,0:T(8,128)S(1)}, f32[8,128]{1,0:T(8,128)S(1)}, u32[]{:S(2)}, u32[]{:S(2)}) collective-permute-start(f32[8,128]{1,0:T(8,128)S(1)} %get-tuple-element.52), channel_id=1, source_target_pairs={{0,8},{1,9},{2,10},{3,11},{4,12},{5,13},{6,14},{7,15},{8,0},{9,1},... | collective-permute-start | bytes 12296 | tf_op jit(solution)/shard_map/ppermute | solution.py:275
  84.7 7.5 %collective-permute-start.15 = (f32[8,128]{1,0:T(8,128)S(1)}, f32[8,128]{1,0:T(8,128)S(1)}, u32[]{:S(2)}, u32[]{:S(2)}) collective-permute-start(f32[8,128]{1,0:T(8,128)S(1)} %bitcast.5), channel_id=1, source_target_pairs={{0,16},{1,17},{2,18},{3,19},{4,20},{5,21},{6,22},{7,23},{8,24},{9,... | collective-permute-start | bytes 12296 | tf_op jit(solution)/shard_map/ppermute | solution.py:280
where the time goes:
time: 93.6 us; the launch traced here: 93.4 us
  waiting for transfers between devices  33.5 us (36%)
  starting transfers between devices  29.2 us (31%)
  Pallas kernels  19.6 us (21%)
  blocking collectives  7.87 us (8%)
  local copies, waits for them, and re-layouts  1.7 us (2%)
  other arithmetic  1.37 us (1%)
    ppermute x11, waiting for transfers between devices, move(): return lax.ppermute(value, AXES, pairs)  21.4 us
    pallas_call x4, Pallas kernels, compare(): pl.pallas_call(functools.partial(compare_kernel, [(block, len(blocks[bloc...  16.5 us
    ppermute x11, starting transfers between devices, move(): return lax.ppermute(value, AXES, pairs)  16.1 us
    ppermute x3, waiting for transfers between devices, climb(): return lax.ppermute(value, AXES, pairs)  9.22 us
    ppermute x2, starting transfers between devices, swap(): return lax.ppermute(value, AXES, pairs)  8.17 us
    all_to_all x1, blocking collectives, exchange(): lax.all_to_all(value, AXES, split_axis=0, concat_axis=0, tiled=True, axis...  7.87 us
    ppermute x3, starting transfers between devices, climb(): return lax.ppermute(value, AXES, pairs)  4.97 us
    ppermute x2, waiting for transfers between devices, swap(): return lax.ppermute(value, AXES, pairs)  2.92 us
  transfers between devices with their start and end apart: 16, of which 10 were waited for; matrix products, arithmetic and copies ran while one was open for 0% of the time, Pallas kernels for 18%

commit v1 on v0

--- a/solution.py
+++ b/solution.py
@@ -14,7 +14,6 @@
 CAPACITY = 96
 EXTRA = 16
 SENT = CAPACITY + EXTRA
-JOINED = CORES * CAPACITY + EXTRA
 BLOCK = GROUPS * CAPACITY
 PART = BLOCK // 2
 FIRST = PART + EXTRA
@@ -32,7 +31,8 @@
     return jnp.concatenate([column_of(row)] * (lanes // 128), axis=1)
 
 
-def prepare_kernel(emb_ref, key_ref, keep_ref, give_ref, place_ref, normed_ref):
+def prepare_kernel(emb_ref, key_ref, *refs):
+    keep_refs, (give_ref, place_ref, normed_ref) = refs[:SIDE], refs[SIDE:]
     labels = key_ref[...] >> 16
     ids = key_ref[...] & 65535
     group = lax.axis_index("group")
@@ -42,42 +42,45 @@
     rank = jnp.sum((before & alike).astype(jnp.int32), axis=0, keepdims=True)
     plane = labels & (SIDE - 1)
     other = (labels >> 2) != core
-    target = plane * SENT + rank
+    turn = (plane - jnp.where(labels < SIDE, z, x)) & (SIDE - 1)
+    target = turn * SENT + rank
 
     def pick(target, count):
         return (lax.broadcasted_iota(jnp.int32, (count, ROWS), 0) == target).astype(jnp.bfloat16)
 
     slot = plane + jnp.where(other, SIDE, 0)
     place_ref[...] = slot * 128 + rank
+    piece = turn + jnp.where(other, SIDE, 0)
     kind = lax.broadcasted_iota(jnp.int32, (8, ROWS), 0)
     digits = jnp.where(kind == 0, ids & 255, jnp.where(kind == 1, ids >> 8, jnp.where(kind == 2, 1, 0)))
-    digits = jnp.concatenate([jnp.where(slot == n, digits, 0) for n in range(GROUPS)], axis=0)
+    digits = jnp.concatenate([jnp.where(piece == n, digits, 0) for n in range(GROUPS)], axis=0)
     lane = jnp.where(labels < SIDE, z, x) * (CORES * CAPACITY) + jnp.where(other, CAPACITY, 0) + rank
     digits = lax.dot_general(digits.astype(jnp.float32).astype(jnp.bfloat16), pick(lane, FEATURES), NT,
                              preferred_element_type=jnp.float32)
     values = emb_ref[...]
     scale = lax.rsqrt(jnp.sum(values * values, axis=1, keepdims=True) + 1e-06)
     normed_ref[...] = (values * scale).astype(jnp.bfloat16)
-    for out_ref, chosen, first in ((give_ref, other, SIDE), (keep_ref, jnp.logical_not(other), 0)):
+    for chosen, first in ((jnp.logical_not(other), 0), (other, SIDE)):
         moved = jnp.dot(pick(jnp.where(chosen, target, -1), SIDE * SENT), normed_ref[...],
-                        preferred_element_type=jnp.float32)
-        out_ref[...] = moved.astype(jnp.bfloat16)
+                        preferred_element_type=jnp.float32).astype(jnp.bfloat16)
         for n in range(SIDE):
+            out_ref, start = (give_ref, n * SENT) if first else (keep_refs[n], 0)
             extra = jnp.concatenate(
                 [digits[8 * (first + n):8 * (first + n) + 8], jnp.zeros((8, FEATURES), jnp.float32)], axis=0)
-            out_ref[n * SENT + CAPACITY:(n + 1) * SENT, :] = extra.astype(jnp.bfloat16)
+            out_ref[start:start + CAPACITY, :] = moved[n * SENT:n * SENT + CAPACITY, :]
+            out_ref[start + CAPACITY:start + SENT, :] = extra.astype(jnp.bfloat16)
 
 
 def prepare(embeddings, keys):
     return pl.pallas_call(
         prepare_kernel,
         out_shape=(
-            jax.ShapeDtypeStruct((SIDE * SENT, FEATURES), jnp.bfloat16),
+            *[jax.ShapeDtypeStruct((SENT, FEATURES), jnp.bfloat16)] * SIDE,
             jax.ShapeDtypeStruct((SIDE * SENT, FEATURES), jnp.bfloat16),
             jax.ShapeDtypeStruct((1, ROWS), jnp.int32),
         ),
         in_specs=[VMEM] * 2,
-        out_specs=(VMEM,) * 3,
+        out_specs=(VMEM,) * (SIDE + 2),
         scratch_shapes=[pltpu.VMEM((ROWS, FEATURES), jnp.bfloat16)],
         compiler_params=pltpu.CompilerParams(vmem_limit_bytes=32 * MIB),
         name="prepare",
@@ -89,36 +92,14 @@
     return jnp.where((group & 1) == 1, lax.axis_index("block") & (SIDE - 1), group >> 1)
 
 
-def join_kernel(keep_ref, got_ref, *out_refs):
-    for n in range(SIDE):
-        start = ((plane() + n) & (SIDE - 1)) * SENT
-        extra = jnp.zeros((EXTRA, FEATURES), jnp.float32)
-        for i, ref in enumerate((keep_ref, got_ref)):
-            rows = ref[pl.ds(pl.multiple_of(start, 16), CAPACITY), :]
-            out_refs[n][i * CAPACITY:(i + 1) * CAPACITY, :] = rows
-            extra = extra + ref[pl.ds(pl.multiple_of(start + CAPACITY, 16), EXTRA), :].astype(jnp.float32)
-        out_refs[n][JOINED - EXTRA:JOINED, :] = extra.astype(jnp.bfloat16)
-
-
-def join(keep, got):
-    return pl.pallas_call(
-        join_kernel,
-        out_shape=(jax.ShapeDtypeStruct((JOINED, FEATURES), jnp.bfloat16),) * SIDE,
-        in_specs=[VMEM] * 2, out_specs=(VMEM,) * SIDE,
-        compiler_params=pltpu.CompilerParams(vmem_limit_bytes=16 * MIB),
-        name="join",
-    )(keep, got)
-
-
 def gather_kernel(*refs):
-    out_ref = refs[SIDE]
+    out_ref = refs[GROUPS]
     extra = jnp.zeros((EXTRA, FEATURES), jnp.float32)
-    size = CORES * CAPACITY
-    for n in range(SIDE):
+    for n in range(GROUPS):
         source = (plane() - n) & (SIDE - 1)
-        start = source * size + (source >> 1) * EXTRA
-        out_ref[pl.ds(pl.multiple_of(start, 16), size), :] = refs[n][0:size, :]
-        extra = extra + refs[n][size:JOINED, :].astype(jnp.float32)
+        start = (source * CORES + n // SIDE) * CAPACITY + (source >> 1) * EXTRA
+        out_ref[pl.ds(pl.multiple_of(start, 16), CAPACITY), :] = refs[n][0:CAPACITY, :]
+        extra = extra + refs[n][CAPACITY:SENT, :].astype(jnp.float32)
     out_ref[PART:FIRST, :] = extra.astype(jnp.bfloat16)
 
 
@@ -126,7 +107,7 @@
     return pl.pallas_call(
         gather_kernel,
         out_shape=jax.ShapeDtypeStruct((BLOCK + EXTRA, FEATURES), jnp.bfloat16),
-        in_specs=[VMEM] * SIDE, out_specs=VMEM,
+        in_specs=[VMEM] * GROUPS, out_specs=VMEM,
         compiler_params=pltpu.CompilerParams(vmem_limit_bytes=16 * MIB),
         name="gather",
     )(*pieces)
@@ -297,9 +278,12 @@
 
 def per_device(embeddings, labels, row_ids):
     keys = labels.reshape(ROWS) * 65536 + row_ids
-    keep, give, place = prepare(embeddings, keys.reshape(1, ROWS))
-    pieces = join(keep, swap(give))
-    own = gather([climb(piece, n) if n else piece for n, piece in enumerate(pieces)])
+    *keep, give, place = prepare(embeddings, keys.reshape(1, ROWS))
+    got = swap(give)
+    kept = [climb(part, n) if n else part for n, part in enumerate(keep)]
+    got = [got[n * SENT:(n + 1) * SENT] for n in range(SIDE)]
+    got = [climb(part, n) if n else part for n, part in enumerate(got)]
+    own = gather(kept + got)
     yp, up, um = move(own, 0, -1), move(own, -1, 0), move(own, 1, 0)
     best = jnp.full((8, BLOCK), -1.0, jnp.float32)
     best, = compare(dict(own=(own,)), best, (("own", (("own", True, False),)),), "compare_own")

time: 93.6 us -> 91.5 us (0.978)
  waiting for transfers between devices: 33.5 us -> 30.1 us
  starting transfers between devices: 29.2 us -> 31.3 us
    ppermute x2, waiting for transfers between devices: 2.92 us -> 0.83 us  [swap(): return lax.ppermute(value, AXES, pairs)]
    ppermute x3 -> x6, starting transfers between devices: 4.97 us -> 7.06 us  [climb(): return lax.ppermute(value, AXES, pairs)]
    ppermute x3 -> x6, waiting for transfers between devices: 9.22 us -> 7.67 us  [climb(): return lax.ppermute(value, AXES, pairs)]
  transfers between devices with their start and end apart: 16 -> 19, of which waited for: 10 -> 11; matrix products, arithmetic and copies ran while one was open for 0% -> 0% of each run, Pallas kernels for 18% -> 18%
where the time goes in v1:
time: 91.5 us; the launch traced here: 91.3 us
  starting transfers between devices  31.3 us (34%)
  waiting for transfers between devices  30.1 us (33%)
  Pallas kernels  19.5 us (21%)
  blocking collectives  7.17 us (8%)
  local copies, waits for them, and re-layouts  1.76 us (2%)
  other arithmetic  1.37 us (1%)
    ppermute x11, waiting for transfers between devices, move(): return lax.ppermute(value, AXES, pairs)  21.6 us
    pallas_call x4, Pallas kernels, compare(): pl.pallas_call(functools.partial(compare_kernel, [(block, len(blocks[bloc...  16.5 us
    ppermute x11, starting transfers between devices, move(): return lax.ppermute(value, AXES, pairs)  16.1 us
    ppermute x2, starting transfers between devices, swap(): return lax.ppermute(value, AXES, pairs)  8.06 us
    ppermute x6, waiting for transfers between devices, climb(): return lax.ppermute(value, AXES, pairs)  7.67 us
    all_to_all x1, blocking collectives, exchange(): lax.all_to_all(value, AXES, split_axis=0, concat_axis=0, tiled=True, axis...  7.17 us
    ppermute x6, starting transfers between devices, climb(): return lax.ppermute(value, AXES, pairs)  7.06 us
  transfers between devices with their start and end apart: 19, of which 11 were waited for; matrix products, arithmetic and copies ran while one was open for 0% of the time, Pallas kernels for 18%

profile of v1, /device:TPU:1, one launch (start us, length us, event | category | flops | bytes accessed | tf_op | source)
XLA Modules:
  0.0 91.3 jit_solution(17705227566743869883)
XLA Ops:
  1.4 1.6 %copy-done = f32[512,1024]{1,0:T(8,128)S(1)} copy-done((f32[512,1024]{1,0:T(8,128)S(1)}, f32[512,1024]{1,0:T(8,128)}, u32[]{:S(2)}) %copy-start) | copy-done | bytes 2097176
  3.0 1.7 %prepare.1 = (bf16[112,1024]{1,0:T(8,128)(2,1)S(1)}, bf16[112,1024]{1,0:T(8,128)(2,1)S(1)}, bf16[112,1024]{1,0:T(8,128)(2,1)S(1)}, bf16[112,1024]{1,0:T(8,128)(2...) custom-call(f32[512,1024]{1,0:T(8,128)S(1)} %copy-done, s32[1,512]{1,0:T(1,128)S(1)} %bitcast.7), custom_call_target="tpu_custom_call" | custom-call | tf_op jit(solution)/shard_map/prepare/pallas_call | solution.py:75
  4.7 1.5 %collective-permute-start.3 = (bf16[448,1024]{1,0:T(8,128)(2,1)S(1)}, bf16[448,1024]{1,0:T(8,128)(2,1)S(1)}, u32[]{:S(2)}, u32[]{:S(2)}) collective-permute-start(bf16[448,1024]{1,0:T(8,128)(2,1)S(1)} %get-tuple-element.33), channel_id=1, source_target_pairs={{0,16},{1,17},{2,18},{3,19},{4,20},{5,21},{6,22},{7,23},{8,24},{9,... | collective-permute-start | bytes 2752520 | tf_op jit(solution)/shard_map/ppermute | solution.py:261
  6.2 1.3 %collective-permute-start = (bf16[112,1024]{1,0:T(8,128)(2,1)S(1)}, bf16[112,1024]{1,0:T(8,128)(2,1)S(1)}, u32[]{:S(2)}, u32[]{:S(2)}) collective-permute-start(bf16[112,1024]{1,0:T(8,128)(2,1)S(1)} %get-tuple-element.30), channel_id=1, source_target_pairs={{0,32},{1,33},{2,34},{3,35},{4,36},{5,37},{6,38},{7,39},{8,40},{9,... | collective-permute-start | bytes 688136 | tf_op jit(solution)/shard_map/ppermute | solution.py:269
  7.5 2.4 %collective-permute-start.1 = (bf16[112,1024]{1,0:T(8,128)(2,1)S(1)}, bf16[112,1024]{1,0:T(8,128)(2,1)S(1)}, u32[]{:S(2)}, u32[]{:S(2)}) collective-permute-start(bf16[112,1024]{1,0:T(8,128)(2,1)S(1)} %get-tuple-element.31), channel_id=1, source_target_pairs={{0,64},{1,65},{2,66},{3,67},{4,68},{5,69},{6,70},{7,71},{8,72},{9,... | collective-permute-start | bytes 688136 | tf_op jit(solution)/shard_map/ppermute | solution.py:269
  11.2 2.1 %collective-permute-start.5 = (bf16[112,1024]{1,0:T(8,128)(2,1)S(1)}, bf16[112,1024]{1,0:T(8,128)(2,1)S(1)}, u32[]{:S(2)}, u32[]{:S(2)}) collective-permute-start(bf16[112,1024]{1,0:T(8,128)(2,1)S(1)} %get-tuple-element.52), channel_id=1, source_target_pairs={{0,64},{1,65},{2,66},{3,67},{4,68},{5,69},{6,70},{7,71},{8,72},{9,... | collective-permute-start | bytes 688136 | tf_op jit(solution)/shard_map/ppermute | solution.py:269
  13.3 2.8 %collective-permute-done.1.refs_2_ = bf16[112,1024]{1,0:T(8,128)(2,1)S(1)} collective-permute-done((bf16[112,1024]{1,0:T(8,128)(2,1)S(1)}, bf16[112,1024]{1,0:T(8,128)(2,1)S(1)}, u32[]{:S(2)}, u32[]{:S(2)}) %collective-permute-start.1) | collective-permute-done | bytes 229408 | tf_op jit(solution)/shard_map/ppermute | solution.py:269
  16.1 2.0 %collective-permute-done.6.refs_7_ = bf16[112,1024]{1,0:T(8,128)(2,1)S(1)} collective-permute-done((bf16[112,1024]{1,0:T(8,128)(2,1)S(1)}, bf16[112,1024]{1,0:T(8,128)(2,1)S(1)}, u32[]{:S(2)}, u32[]{:S(2)}) %collective-permute-start.6) | collective-permute-done | bytes 229408 | tf_op jit(solution)/shard_map/ppermute | solution.py:269
  18.5 2.5 %collective-permute-done.4.refs_5_ = bf16[112,1024]{1,0:T(8,128)(2,1)S(1)} collective-permute-done((bf16[112,1024]{1,0:T(8,128)(2,1)S(1)}, bf16[112,1024]{1,0:T(8,128)(2,1)S(1)}, u32[]{:S(2)}, u32[]{:S(2)}) %collective-permute-start.4) | collective-permute-done | bytes 229408 | tf_op jit(solution)/shard_map/ppermute | solution.py:269
  21.1 1.4 %collective-permute-start.7 = (bf16[784,1024]{1,0:T(8,128)(2,1)S(1)}, bf16[784,1024]{1,0:T(8,128)(2,1)S(1)}, u32[]{:S(2)}, u32[]{:S(2)}) collective-permute-start(bf16[784,1024]{1,0:T(8,128)(2,1)S(1)} %gather.1.refs_0_.refs_1_), channel_id=1, source_target_pairs={{0,12},{1,13},{2,14},{3,15},{4,0},{5,1},{6,2},{7,3},{8,4},{9,5},{1... | collective-permute-start | bytes 4816904 | tf_op jit(solution)/shard_map/ppermute | solution.py:256
  22.5 3.8 %collective-permute-start.8 = (bf16[784,1024]{1,0:T(8,128)(2,1)S(1)}, bf16[784,1024]{1,0:T(8,128)(2,1)S(1)}, u32[]{:S(2)}, u32[]{:S(2)}) collective-permute-start(bf16[784,1024]{1,0:T(8,128)(2,1)S(1)} %gather.1.refs_0_.refs_1_), channel_id=1, source_target_pairs={{0,3},{1,0},{2,1},{3,2},{4,7},{5,4},{6,5},{7,6},{8,11},{9,8},{10,9... | collective-permute-start | bytes 4816904 | tf_op jit(solution)/shard_map/ppermute | solution.py:256
  26.3 1.7 %compare_own.1.before_ref = f32[8,768]{1,0:T(8,128)S(1)} custom-call(f32[8,768]{1,0:T(8,128)S(1)} %broadcast_in_dim.3.before_ref, bf16[784,1024]{1,0:T(8,128)(2,1)S(1)} %gather.1.refs_0_.refs_1_), custom_call_target="tpu_custom_call" | custom-call | flops 1207959552 | bytes 1572864 | tf_op jit(solution)/shard_map/compare_own/pallas_call | solution.py:216
  28.0 14.4 %collective-permute-done.7.refs_2_.refs_3_ = bf16[784,1024]{1,0:T(8,128)(2,1)S(1)} collective-permute-done((bf16[784,1024]{1,0:T(8,128)(2,1)S(1)}, bf16[784,1024]{1,0:T(8,128)(2,1)S(1)}, u32[]{:S(2)}, u32[]{:S(2)}) %collective-permute-start.7) | collective-permute-done | bytes 1605664 | tf_op jit(solution)/shard_map/ppermute | solution.py:256
  42.4 1.6 %collective-permute-done.8.refs_1_.refs_2_ = bf16[784,1024]{1,0:T(8,128)(2,1)S(1)} collective-permute-done((bf16[784,1024]{1,0:T(8,128)(2,1)S(1)}, bf16[784,1024]{1,0:T(8,128)(2,1)S(1)}, u32[]{:S(2)}, u32[]{:S(2)}) %collective-permute-start.8) | collective-permute-done | bytes 1605664 | tf_op jit(solution)/shard_map/ppermute | solution.py:256
  44.0 3.5 %collective-permute-start.11 = (bf16[400,1024]{1,0:T(8,128)(2,1)S(1)}, bf16[400,1024]{1,0:T(8,128)(2,1)S(1)}, u32[]{:S(2)}, u32[]{:S(2)}) collective-permute-start(bf16[400,1024]{1,0:T(8,128)(2,1)S(1)} %slice.28), channel_id=1, source_target_pairs={{0,3},{1,0},{2,1},{3,2},{4,7},{5,4},{6,5},{7,6},{8,11},{9,8},{10,9... | collective-permute-start | bytes 2457608 | tf_op jit(solution)/shard_map/ppermute | solution.py:256
  47.8 6.3 %compare_near.1 = (f32[8,768]{1,0:T(8,128)S(1)}, f32[8,128]{1,0:T(8,128)S(1)}) custom-call(f32[8,768]{1,0:T(8,128)S(1)} %compare_own.1.before_ref, bf16[784,1024]{1,0:T(8,128)(2,1)S(1)} %gather.1.refs_0_.refs_1_, bf16[784,1024]{1,0:T(8,128)(2,1)S(1)} %collective-permute-done.8.refs_1_.refs_2_, bf16[784,1024]{1,0:T(8,128)(2,1)S(1)} %collective-permute-done.7.refs_2_.refs_3_, ...), custom_call_target="tpu_custom_call" | custom-call | flops 4831838208 | bytes 1572864 | tf_op jit(solution)/shard_map/compare_near/pallas_call | solution.py:216
  54.2 2.8 %collective-permute-start.10 = (f32[8,128]{1,0:T(8,128)S(1)}, f32[8,128]{1,0:T(8,128)S(1)}, u32[]{:S(2)}, u32[]{:S(2)}) collective-permute-start(f32[8,128]{1,0:T(8,128)S(1)} %get-tuple-element.36), channel_id=1, source_target_pairs={{0,3},{1,0},{2,1},{3,2},{4,7},{5,4},{6,5},{7,6},{8,11},{9,8},{10,9... | collective-permute-start | bytes 12296 | tf_op jit(solution)/shard_map/ppermute | solution.py:256
  57.7 2.5 %collective-permute-done.12.refs_2_.refs_4_ = bf16[384,1024]{1,0:T(8,128)(2,1)S(1)} collective-permute-done((bf16[384,1024]{1,0:T(8,128)(2,1)S(1)}, bf16[384,1024]{1,0:T(8,128)(2,1)S(1)}, u32[]{:S(2)}, u32[]{:S(2)}) %collective-permute-start.12) | collective-permute-done | bytes 786464 | tf_op jit(solution)/shard_map/ppermute | solution.py:256
  60.2 3.6 %compare_line.1 = (f32[8,768]{1,0:T(8,128)S(1)}, f32[8,128]{1,0:T(8,128)S(1)}, f32[8,128]{1,0:T(8,128)S(1)}) custom-call(f32[8,768]{1,0:T(8,128)S(1)} %get-tuple-element.38.before_ref, bf16[784,1024]{1,0:T(8,128)(2,1)S(1)} %gather.1.refs_0_.refs_1_, bf16[400,1024]{1,0:T(8,128)(2,1)S(1)} %collective-permute-done.11.refs_1_.refs_3_, ...), custom_call_target="tpu_custom_call" | custom-call | flops 2415919104 | bytes 1572864 | tf_op jit(solution)/shard_map/compare_line/pallas_call | solution.py:216
  63.8 1.8 %collective-permute-start.15 = (f32[8,128]{1,0:T(8,128)S(1)}, f32[8,128]{1,0:T(8,128)S(1)}, u32[]{:S(2)}, u32[]{:S(2)}) collective-permute-start(f32[8,128]{1,0:T(8,128)S(1)} %get-tuple-element.45), channel_id=1, source_target_pairs={{0,4},{1,5},{2,6},{3,7},{4,8},{5,9},{6,10},{7,11},{8,12},{9,13},{1... | collective-permute-start | bytes 12296 | tf_op jit(solution)/shard_map/ppermute | solution.py:256
  65.6 4.9 %compare_far.1 = (f32[8,768]{1,0:T(8,128)}, f32[8,128]{1,0:T(8,128)S(1)}, f32[8,128]{1,0:T(8,128)S(1)}, f32[8,128]{1,0:T(8,128)S(1)}) custom-call(f32[8,768]{1,0:T(8,128)S(1)} %get-tuple-element.39.before_ref, bf16[784,1024]{1,0:T(8,128)(2,1)S(1)} %collective-permute-done.13.refs_0_, bf16[784,1024]{1,0:T(8,128)(2,1)S(1)} %gather.1.refs_0_.refs_1_, ...), custom_call_target="tpu_custom_call" | custom-call | flops 3623878656 | bytes 1572864 | tf_op jit(solution)/shard_map/compare_far/pallas_call | solution.py:216
  71.6 1.6 %collective-permute-start.17 = (f32[8,128]{1,0:T(8,128)S(1)}, f32[8,128]{1,0:T(8,128)S(1)}, u32[]{:S(2)}, u32[]{:S(2)}) collective-permute-start(f32[8,128]{1,0:T(8,128)S(1)} %get-tuple-element.50), channel_id=1, source_target_pairs={{0,8},{1,9},{2,10},{3,11},{4,12},{5,13},{6,14},{7,15},{8,0},{9,1},... | collective-permute-start | bytes 12296 | tf_op jit(solution)/shard_map/ppermute | solution.py:256
  75.6 7.2 %all_to_all.11 = f32[4,2,128]{2,1,0:T(2,128)S(1)} all-to-all(f32[4,2,128]{2,1,0:T(2,128)S(1)} %bitcast.8), channel_id=1, replica_groups={{0,32,64,96},{4,36,68,100},{8,40,72,104},{12,44,76,108},{1,33,65,97},{5..., dimensions={0} | all-to-all | bytes 8192 | tf_op jit(solution)/shard_map/all_to_all | solution.py:276
  82.8 6.6 %collective-permute-start.18 = (f32[8,128]{1,0:T(8,128)S(1)}, f32[8,128]{1,0:T(8,128)S(1)}, u32[]{:S(2)}, u32[]{:S(2)}) collective-permute-start(f32[8,128]{1,0:T(8,128)S(1)} %bitcast.5), channel_id=1, source_target_pairs={{0,16},{1,17},{2,18},{3,19},{4,20},{5,21},{6,22},{7,23},{8,24},{9,... | collective-permute-start | bytes 12296 | tf_op jit(solution)/shard_map/ppermute | solution.py:261
  (31 shorter events, 9.9 us)
Async XLA Ops:
  1.4 1.6 %copy-start = (f32[512,1024]{1,0:T(8,128)S(1)}, f32[512,1024]{1,0:T(8,128)}, u32[]{:S(2)}) copy-start(f32[512,1024]{1,0:T(8,128)} %emb_ref.1) | copy-start | bytes 6291460
  4.7 6.4 %collective-permute-start.3 = (bf16[448,1024]{1,0:T(8,128)(2,1)S(1)}, bf16[448,1024]{1,0:T(8,128)(2,1)S(1)}, u32[]{:S(2)}, u32[]{:S(2)}) collective-permute-start(bf16[448,1024]{1,0:T(8,128)(2,1)S(1)} %get-tuple-element.33), channel_id=1, source_target_pairs={{0,16},{1,17},{2,18},{3,19},{4,20},{5,21},{6,22},{7,23},{8,24},{9,... | collective-permute-start | bytes 2752520 | tf_op jit(solution)/shard_map/ppermute | solution.py:261
  6.2 7.1 %collective-permute-start = (bf16[112,1024]{1,0:T(8,128)(2,1)S(1)}, bf16[112,1024]{1,0:T(8,128)(2,1)S(1)}, u32[]{:S(2)}, u32[]{:S(2)}) collective-permute-start(bf16[112,1024]{1,0:T(8,128)(2,1)S(1)} %get-tuple-element.30), channel_id=1, source_target_pairs={{0,32},{1,33},{2,34},{3,35},{4,36},{5,37},{6,38},{7,39},{8,40},{9,... | collective-permute-start | bytes 688136 | tf_op jit(solution)/shard_map/ppermute | solution.py:269
  7.5 8.6 %collective-permute-start.1 = (bf16[112,1024]{1,0:T(8,128)(2,1)S(1)}, bf16[112,1024]{1,0:T(8,128)(2,1)S(1)}, u32[]{:S(2)}, u32[]{:S(2)}) collective-permute-start(bf16[112,1024]{1,0:T(8,128)(2,1)S(1)} %get-tuple-element.31), channel_id=1, source_target_pairs={{0,64},{1,65},{2,66},{3,67},{4,68},{5,69},{6,70},{7,71},{8,72},{9,... | collective-permute-start | bytes 688136 | tf_op jit(solution)/shard_map/ppermute | solution.py:269
  9.9 6.2 %collective-permute-start.2 = (bf16[112,1024]{1,0:T(8,128)(2,1)S(1)}, bf16[112,1024]{1,0:T(8,128)(2,1)S(1)}, u32[]{:S(2)}, u32[]{:S(2)}) collective-permute-start(bf16[112,1024]{1,0:T(8,128)(2,1)S(1)} %get-tuple-element.32), channel_id=1, source_target_pairs={{0,96},{1,97},{2,98},{3,99},{4,100},{5,101},{6,102},{7,103},{8,104... | collective-permute-start | bytes 688136 | tf_op jit(solution)/shard_map/ppermute | solution.py:269
  11.1 6.9 %collective-permute-start.6 = (bf16[112,1024]{1,0:T(8,128)(2,1)S(1)}, bf16[112,1024]{1,0:T(8,128)(2,1)S(1)}, u32[]{:S(2)}, u32[]{:S(2)}) collective-permute-start(bf16[112,1024]{1,0:T(8,128)(2,1)S(1)} %get-tuple-element.51), channel_id=1, source_target_pairs={{0,96},{1,97},{2,98},{3,99},{4,100},{5,101},{6,102},{7,103},{8,104... | collective-permute-start | bytes 688136 | tf_op jit(solution)/shard_map/ppermute | solution.py:269
  11.2 7.3 %collective-permute-start.5 = (bf16[112,1024]{1,0:T(8,128)(2,1)S(1)}, bf16[112,1024]{1,0:T(8,128)(2,1)S(1)}, u32[]{:S(2)}, u32[]{:S(2)}) collective-permute-start(bf16[112,1024]{1,0:T(8,128)(2,1)S(1)} %get-tuple-element.52), channel_id=1, source_target_pairs={{0,64},{1,65},{2,66},{3,67},{4,68},{5,69},{6,70},{7,71},{8,72},{9,... | collective-permute-start | bytes 688136 | tf_op jit(solution)/shard_map/ppermute | solution.py:269
  13.3 7.7 %collective-permute-start.4 = (bf16[112,1024]{1,0:T(8,128)(2,1)S(1)}, bf16[112,1024]{1,0:T(8,128)(2,1)S(1)}, u32[]{:S(2)}, u32[]{:S(2)}) collective-permute-start(bf16[112,1024]{1,0:T(8,128)(2,1)S(1)} %get-tuple-element.53), channel_id=1, source_target_pairs={{0,32},{1,33},{2,34},{3,35},{4,36},{5,37},{6,38},{7,39},{8,40},{9,... | collective-permute-start | bytes 688136 | tf_op jit(solution)/shard_map/ppermute | solution.py:269
  21.1 21.3 %collective-permute-start.7 = (bf16[784,1024]{1,0:T(8,128)(2,1)S(1)}, bf16[784,1024]{1,0:T(8,128)(2,1)S(1)}, u32[]{:S(2)}, u32[]{:S(2)}) collective-permute-start(bf16[784,1024]{1,0:T(8,128)(2,1)S(1)} %gather.1.refs_0_.refs_1_), channel_id=1, source_target_pairs={{0,12},{1,13},{2,14},{3,15},{4,0},{5,1},{6,2},{7,3},{8,4},{9,5},{1... | collective-permute-start | bytes 4816904 | tf_op jit(solution)/shard_map/ppermute | solution.py:256
  22.5 21.5 %collective-permute-start.8 = (bf16[784,1024]{1,0:T(8,128)(2,1)S(1)}, bf16[784,1024]{1,0:T(8,128)(2,1)S(1)}, u32[]{:S(2)}, u32[]{:S(2)}) collective-permute-start(bf16[784,1024]{1,0:T(8,128)(2,1)S(1)} %gather.1.refs_0_.refs_1_), channel_id=1, source_target_pairs={{0,3},{1,0},{2,1},{3,2},{4,7},{5,4},{6,5},{7,6},{8,11},{9,8},{10,9... | collective-permute-start | bytes 4816904 | tf_op jit(solution)/shard_map/ppermute | solution.py:256
  26.3 21.3 %collective-permute-start.9 = (bf16[784,1024]{1,0:T(8,128)(2,1)S(1)}, bf16[784,1024]{1,0:T(8,128)(2,1)S(1)}, u32[]{:S(2)}, u32[]{:S(2)}) collective-permute-start(bf16[784,1024]{1,0:T(8,128)(2,1)S(1)} %gather.1.refs_0_.refs_1_), channel_id=1, source_target_pairs={{0,1},{1,2},{2,3},{3,0},{4,5},{5,6},{6,7},{7,4},{8,9},{9,10},{10,1... | collective-permute-start | bytes 4816904 | tf_op jit(solution)/shard_map/ppermute | solution.py:256
  42.4 23.2 %collective-permute-start.13 = (bf16[784,1024]{1,0:T(8,128)(2,1)S(1)}, bf16[784,1024]{1,0:T(8,128)(2,1)S(1)}, u32[]{:S(2)}, u32[]{:S(2)}) collective-permute-start(bf16[784,1024]{1,0:T(8,128)(2,1)S(1)} %collective-permute-done.7.refs_2_.refs_3_), channel_id=1, source_target_pairs={{0,12},{1,13},{2,14},{3,15},{4,0},{5,1},{6,2},{7,3},{8,4},{9,5},{1... | collective-permute-start | bytes 4816904 | tf_op jit(solution)/shard_map/ppermute | solution.py:256
  44.0 16.1 %collective-permute-start.11 = (bf16[400,1024]{1,0:T(8,128)(2,1)S(1)}, bf16[400,1024]{1,0:T(8,128)(2,1)S(1)}, u32[]{:S(2)}, u32[]{:S(2)}) collective-permute-start(bf16[400,1024]{1,0:T(8,128)(2,1)S(1)} %slice.28), channel_id=1, source_target_pairs={{0,3},{1,0},{2,1},{3,2},{4,7},{5,4},{6,5},{7,6},{8,11},{9,8},{10,9... | collective-permute-start | bytes 2457608 | tf_op jit(solution)/shard_map/ppermute | solution.py:256
  47.6 12.6 %collective-permute-start.12 = (bf16[384,1024]{1,0:T(8,128)(2,1)S(1)}, bf16[384,1024]{1,0:T(8,128)(2,1)S(1)}, u32[]{:S(2)}, u32[]{:S(2)}) collective-permute-start(bf16[384,1024]{1,0:T(8,128)(2,1)S(1)} %slice.29), channel_id=1, source_target_pairs={{0,1},{1,2},{2,3},{3,0},{4,5},{5,6},{6,7},{7,4},{8,9},{9,10},{10,1... | collective-permute-start | bytes 2359304 | tf_op jit(solution)/shard_map/ppermute | solution.py:256
  54.2 3.5 %collective-permute-start.10 = (f32[8,128]{1,0:T(8,128)S(1)}, f32[8,128]{1,0:T(8,128)S(1)}, u32[]{:S(2)}, u32[]{:S(2)}) collective-permute-start(f32[8,128]{1,0:T(8,128)S(1)} %get-tuple-element.36), channel_id=1, source_target_pairs={{0,3},{1,0},{2,1},{3,2},{4,7},{5,4},{6,5},{7,6},{8,11},{9,8},{10,9... | collective-permute-start | bytes 12296 | tf_op jit(solution)/shard_map/ppermute | solution.py:256
  63.7 6.8 %collective-permute-start.14 = (f32[8,128]{1,0:T(8,128)S(1)}, f32[8,128]{1,0:T(8,128)S(1)}, u32[]{:S(2)}, u32[]{:S(2)}) collective-permute-start(f32[8,128]{1,0:T(8,128)S(1)} %get-tuple-element.44), channel_id=1, source_target_pairs={{0,2},{1,3},{2,0},{3,1},{4,6},{5,7},{6,4},{7,5},{8,10},{9,11},{10,... | collective-permute-start | bytes 12296 | tf_op jit(solution)/shard_map/ppermute | solution.py:256
  63.8 6.7 %collective-permute-start.15 = (f32[8,128]{1,0:T(8,128)S(1)}, f32[8,128]{1,0:T(8,128)S(1)}, u32[]{:S(2)}, u32[]{:S(2)}) collective-permute-start(f32[8,128]{1,0:T(8,128)S(1)} %get-tuple-element.45), channel_id=1, source_target_pairs={{0,4},{1,5},{2,6},{3,7},{4,8},{5,9},{6,10},{7,11},{8,12},{9,13},{1... | collective-permute-start | bytes 12296 | tf_op jit(solution)/shard_map/ppermute | solution.py:256
  70.6 3.7 %collective-permute-start.16 = (f32[8,128]{1,0:T(8,128)S(1)}, f32[8,128]{1,0:T(8,128)S(1)}, u32[]{:S(2)}, u32[]{:S(2)}) collective-permute-start(f32[8,128]{1,0:T(8,128)S(1)} %get-tuple-element.49), channel_id=1, source_target_pairs={{0,1},{1,2},{2,3},{3,0},{4,5},{5,6},{6,7},{7,4},{8,9},{9,10},{10,1... | collective-permute-start | bytes 12296 | tf_op jit(solution)/shard_map/ppermute | solution.py:256
  71.6 4.0 %collective-permute-start.17 = (f32[8,128]{1,0:T(8,128)S(1)}, f32[8,128]{1,0:T(8,128)S(1)}, u32[]{:S(2)}, u32[]{:S(2)}) collective-permute-start(f32[8,128]{1,0:T(8,128)S(1)} %get-tuple-element.50), channel_id=1, source_target_pairs={{0,8},{1,9},{2,10},{3,11},{4,12},{5,13},{6,14},{7,15},{8,0},{9,1},... | collective-permute-start | bytes 12296 | tf_op jit(solution)/shard_map/ppermute | solution.py:256
  82.8 7.4 %collective-permute-start.18 = (f32[8,128]{1,0:T(8,128)S(1)}, f32[8,128]{1,0:T(8,128)S(1)}, u32[]{:S(2)}, u32[]{:S(2)}) collective-permute-start(f32[8,128]{1,0:T(8,128)S(1)} %bitcast.5), channel_id=1, source_target_pairs={{0,16},{1,17},{2,18},{3,19},{4,20},{5,21},{6,22},{7,23},{8,24},{9,... | collective-permute-start | bytes 12296 | tf_op jit(solution)/shard_map/ppermute | solution.py:261

commit v2 on v1

--- a/solution.py
+++ b/solution.py
@@ -171,7 +171,7 @@
     out_refs, (held, sems) = refs[:-2], refs[-2:]
     whole = Whole([sources[columns] for columns, _ in products], held, sems)
     extras = {block: refs_of[0][PART:FIRST, :] for block, refs_of in sources.items()}
-    found = {}
+    found, row_keys_of = {}, {}
 
     def note(name, values):
         found[name] = jnp.maximum(found[name], values) if name in found else values
@@ -181,7 +181,9 @@
         columns_best = jnp.full((8, BLOCK), -1.0, jnp.float32)
         whole.wait(i)
         for rows, for_rows, for_columns in uses:
-            keys = row_keys(extras[rows])
+            if rows not in row_keys_of:
+                row_keys_of[rows] = row_keys(extras[rows])
+            keys = row_keys_of[rows]
             rows_best = []
             for part, r in zip(halves(sources[rows]), (0, PART)):
                 own = jnp.concatenate([keys[r:r + PART, :]] * (BLOCK // 128), axis=1)

time: 91.5 us -> 91.5 us (level)
  no operation moved by 1% of the time
where the time goes in v2:
time: 91.5 us; the launch traced here: 91.3 us
  starting transfers between devices  31.3 us (34%)
  waiting for transfers between devices  30.1 us (33%)
  Pallas kernels  19.5 us (21%)
  blocking collectives  7.17 us (8%)
  local copies, waits for them, and re-layouts  1.76 us (2%)
  other arithmetic  1.37 us (1%)
    ppermute x11, waiting for transfers between devices, move(): return lax.ppermute(value, AXES, pairs)  21.6 us
    pallas_call x4, Pallas kernels, compare(): pl.pallas_call(functools.partial(compare_kernel, [(block, len(blocks[bloc...  16.5 us
    ppermute x11, starting transfers between devices, move(): return lax.ppermute(value, AXES, pairs)  16.1 us
    ppermute x2, starting transfers between devices, swap(): return lax.ppermute(value, AXES, pairs)  8.06 us
    ppermute x6, waiting for transfers between devices, climb(): return lax.ppermute(value, AXES, pairs)  7.67 us
    all_to_all x1, blocking collectives, exchange(): lax.all_to_all(value, AXES, split_axis=0, concat_axis=0, tiled=True, axis...  7.17 us
    ppermute x6, starting transfers between devices, climb(): return lax.ppermute(value, AXES, pairs)  7.06 us
  transfers between devices with their start and end apart: 19, of which 11 were waited for; matrix products, arithmetic and copies ran while one was open for 0% of the time, Pallas kernels for 18%

profile of v2, /device:TPU:1, one launch (start us, length us, event | category | flops | bytes accessed | tf_op | source)
XLA Modules:
  0.0 91.3 jit_solution(17705227566743869883)
XLA Ops:
  1.4 1.6 %copy-done = f32[512,1024]{1,0:T(8,128)S(1)} copy-done((f32[512,1024]{1,0:T(8,128)S(1)}, f32[512,1024]{1,0:T(8,128)}, u32[]{:S(2)}) %copy-start) | copy-done | bytes 2097176
  3.0 1.7 %prepare.1 = (bf16[112,1024]{1,0:T(8,128)(2,1)S(1)}, bf16[112,1024]{1,0:T(8,128)(2,1)S(1)}, bf16[112,1024]{1,0:T(8,128)(2,1)S(1)}, bf16[112,1024]{1,0:T(8,128)(2...) custom-call(f32[512,1024]{1,0:T(8,128)S(1)} %copy-done, s32[1,512]{1,0:T(1,128)S(1)} %bitcast.7), custom_call_target="tpu_custom_call" | custom-call | tf_op jit(solution)/shard_map/prepare/pallas_call | solution.py:75
  4.7 1.5 %collective-permute-start.3 = (bf16[448,1024]{1,0:T(8,128)(2,1)S(1)}, bf16[448,1024]{1,0:T(8,128)(2,1)S(1)}, u32[]{:S(2)}, u32[]{:S(2)}) collective-permute-start(bf16[448,1024]{1,0:T(8,128)(2,1)S(1)} %get-tuple-element.33), channel_id=1, source_target_pairs={{0,16},{1,17},{2,18},{3,19},{4,20},{5,21},{6,22},{7,23},{8,24},{9,... | collective-permute-start | bytes 2752520 | tf_op jit(solution)/shard_map/ppermute | solution.py:263
  6.2 1.3 %collective-permute-start = (bf16[112,1024]{1,0:T(8,128)(2,1)S(1)}, bf16[112,1024]{1,0:T(8,128)(2,1)S(1)}, u32[]{:S(2)}, u32[]{:S(2)}) collective-permute-start(bf16[112,1024]{1,0:T(8,128)(2,1)S(1)} %get-tuple-element.30), channel_id=1, source_target_pairs={{0,32},{1,33},{2,34},{3,35},{4,36},{5,37},{6,38},{7,39},{8,40},{9,... | collective-permute-start | bytes 688136 | tf_op jit(solution)/shard_map/ppermute | solution.py:271
  7.5 2.4 %collective-permute-start.1 = (bf16[112,1024]{1,0:T(8,128)(2,1)S(1)}, bf16[112,1024]{1,0:T(8,128)(2,1)S(1)}, u32[]{:S(2)}, u32[]{:S(2)}) collective-permute-start(bf16[112,1024]{1,0:T(8,128)(2,1)S(1)} %get-tuple-element.31), channel_id=1, source_target_pairs={{0,64},{1,65},{2,66},{3,67},{4,68},{5,69},{6,70},{7,71},{8,72},{9,... | collective-permute-start | bytes 688136 | tf_op jit(solution)/shard_map/ppermute | solution.py:271
  11.2 2.1 %collective-permute-start.5 = (bf16[112,1024]{1,0:T(8,128)(2,1)S(1)}, bf16[112,1024]{1,0:T(8,128)(2,1)S(1)}, u32[]{:S(2)}, u32[]{:S(2)}) collective-permute-start(bf16[112,1024]{1,0:T(8,128)(2,1)S(1)} %get-tuple-element.52), channel_id=1, source_target_pairs={{0,64},{1,65},{2,66},{3,67},{4,68},{5,69},{6,70},{7,71},{8,72},{9,... | collective-permute-start | bytes 688136 | tf_op jit(solution)/shard_map/ppermute | solution.py:271
  13.3 2.8 %collective-permute-done.1.refs_2_ = bf16[112,1024]{1,0:T(8,128)(2,1)S(1)} collective-permute-done((bf16[112,1024]{1,0:T(8,128)(2,1)S(1)}, bf16[112,1024]{1,0:T(8,128)(2,1)S(1)}, u32[]{:S(2)}, u32[]{:S(2)}) %collective-permute-start.1) | collective-permute-done | bytes 229408 | tf_op jit(solution)/shard_map/ppermute | solution.py:271
  16.1 2.0 %collective-permute-done.6.refs_7_ = bf16[112,1024]{1,0:T(8,128)(2,1)S(1)} collective-permute-done((bf16[112,1024]{1,0:T(8,128)(2,1)S(1)}, bf16[112,1024]{1,0:T(8,128)(2,1)S(1)}, u32[]{:S(2)}, u32[]{:S(2)}) %collective-permute-start.6) | collective-permute-done | bytes 229408 | tf_op jit(solution)/shard_map/ppermute | solution.py:271
  18.5 2.5 %collective-permute-done.4.refs_5_ = bf16[112,1024]{1,0:T(8,128)(2,1)S(1)} collective-permute-done((bf16[112,1024]{1,0:T(8,128)(2,1)S(1)}, bf16[112,1024]{1,0:T(8,128)(2,1)S(1)}, u32[]{:S(2)}, u32[]{:S(2)}) %collective-permute-start.4) | collective-permute-done | bytes 229408 | tf_op jit(solution)/shard_map/ppermute | solution.py:271
  21.1 1.4 %collective-permute-start.7 = (bf16[784,1024]{1,0:T(8,128)(2,1)S(1)}, bf16[784,1024]{1,0:T(8,128)(2,1)S(1)}, u32[]{:S(2)}, u32[]{:S(2)}) collective-permute-start(bf16[784,1024]{1,0:T(8,128)(2,1)S(1)} %gather.1.refs_0_.refs_1_), channel_id=1, source_target_pairs={{0,12},{1,13},{2,14},{3,15},{4,0},{5,1},{6,2},{7,3},{8,4},{9,5},{1... | collective-permute-start | bytes 4816904 | tf_op jit(solution)/shard_map/ppermute | solution.py:258
  22.5 3.8 %collective-permute-start.8 = (bf16[784,1024]{1,0:T(8,128)(2,1)S(1)}, bf16[784,1024]{1,0:T(8,128)(2,1)S(1)}, u32[]{:S(2)}, u32[]{:S(2)}) collective-permute-start(bf16[784,1024]{1,0:T(8,128)(2,1)S(1)} %gather.1.refs_0_.refs_1_), channel_id=1, source_target_pairs={{0,3},{1,0},{2,1},{3,2},{4,7},{5,4},{6,5},{7,6},{8,11},{9,8},{10,9... | collective-permute-start | bytes 4816904 | tf_op jit(solution)/shard_map/ppermute | solution.py:258
  26.3 1.7 %compare_own.1.before_ref = f32[8,768]{1,0:T(8,128)S(1)} custom-call(f32[8,768]{1,0:T(8,128)S(1)} %broadcast_in_dim.3.before_ref, bf16[784,1024]{1,0:T(8,128)(2,1)S(1)} %gather.1.refs_0_.refs_1_), custom_call_target="tpu_custom_call" | custom-call | flops 1207959552 | bytes 1572864 | tf_op jit(solution)/shard_map/compare_own/pallas_call | solution.py:218
  28.0 14.4 %collective-permute-done.7.refs_2_.refs_3_ = bf16[784,1024]{1,0:T(8,128)(2,1)S(1)} collective-permute-done((bf16[784,1024]{1,0:T(8,128)(2,1)S(1)}, bf16[784,1024]{1,0:T(8,128)(2,1)S(1)}, u32[]{:S(2)}, u32[]{:S(2)}) %collective-permute-start.7) | collective-permute-done | bytes 1605664 | tf_op jit(solution)/shard_map/ppermute | solution.py:258
  42.4 1.6 %collective-permute-done.8.refs_1_.refs_2_ = bf16[784,1024]{1,0:T(8,128)(2,1)S(1)} collective-permute-done((bf16[784,1024]{1,0:T(8,128)(2,1)S(1)}, bf16[784,1024]{1,0:T(8,128)(2,1)S(1)}, u32[]{:S(2)}, u32[]{:S(2)}) %collective-permute-start.8) | collective-permute-done | bytes 1605664 | tf_op jit(solution)/shard_map/ppermute | solution.py:258
  44.0 3.5 %collective-permute-start.11 = (bf16[400,1024]{1,0:T(8,128)(2,1)S(1)}, bf16[400,1024]{1,0:T(8,128)(2,1)S(1)}, u32[]{:S(2)}, u32[]{:S(2)}) collective-permute-start(bf16[400,1024]{1,0:T(8,128)(2,1)S(1)} %slice.28), channel_id=1, source_target_pairs={{0,3},{1,0},{2,1},{3,2},{4,7},{5,4},{6,5},{7,6},{8,11},{9,8},{10,9... | collective-permute-start | bytes 2457608 | tf_op jit(solution)/shard_map/ppermute | solution.py:258
  47.8 6.3 %compare_near.1 = (f32[8,768]{1,0:T(8,128)S(1)}, f32[8,128]{1,0:T(8,128)S(1)}) custom-call(f32[8,768]{1,0:T(8,128)S(1)} %compare_own.1.before_ref, bf16[784,1024]{1,0:T(8,128)(2,1)S(1)} %gather.1.refs_0_.refs_1_, bf16[784,1024]{1,0:T(8,128)(2,1)S(1)} %collective-permute-done.8.refs_1_.refs_2_, bf16[784,1024]{1,0:T(8,128)(2,1)S(1)} %collective-permute-done.7.refs_2_.refs_3_, ...), custom_call_target="tpu_custom_call" | custom-call | flops 4831838208 | bytes 1572864 | tf_op jit(solution)/shard_map/compare_near/pallas_call | solution.py:218
  54.2 2.8 %collective-permute-start.10 = (f32[8,128]{1,0:T(8,128)S(1)}, f32[8,128]{1,0:T(8,128)S(1)}, u32[]{:S(2)}, u32[]{:S(2)}) collective-permute-start(f32[8,128]{1,0:T(8,128)S(1)} %get-tuple-element.36), channel_id=1, source_target_pairs={{0,3},{1,0},{2,1},{3,2},{4,7},{5,4},{6,5},{7,6},{8,11},{9,8},{10,9... | collective-permute-start | bytes 12296 | tf_op jit(solution)/shard_map/ppermute | solution.py:258
  57.7 2.5 %collective-permute-done.12.refs_2_.refs_4_ = bf16[384,1024]{1,0:T(8,128)(2,1)S(1)} collective-permute-done((bf16[384,1024]{1,0:T(8,128)(2,1)S(1)}, bf16[384,1024]{1,0:T(8,128)(2,1)S(1)}, u32[]{:S(2)}, u32[]{:S(2)}) %collective-permute-start.12) | collective-permute-done | bytes 786464 | tf_op jit(solution)/shard_map/ppermute | solution.py:258
  60.2 3.6 %compare_line.1 = (f32[8,768]{1,0:T(8,128)S(1)}, f32[8,128]{1,0:T(8,128)S(1)}, f32[8,128]{1,0:T(8,128)S(1)}) custom-call(f32[8,768]{1,0:T(8,128)S(1)} %get-tuple-element.38.before_ref, bf16[784,1024]{1,0:T(8,128)(2,1)S(1)} %gather.1.refs_0_.refs_1_, bf16[400,1024]{1,0:T(8,128)(2,1)S(1)} %collective-permute-done.11.refs_1_.refs_3_, ...), custom_call_target="tpu_custom_call" | custom-call | flops 2415919104 | bytes 1572864 | tf_op jit(solution)/shard_map/compare_line/pallas_call | solution.py:218
  63.8 1.8 %collective-permute-start.15 = (f32[8,128]{1,0:T(8,128)S(1)}, f32[8,128]{1,0:T(8,128)S(1)}, u32[]{:S(2)}, u32[]{:S(2)}) collective-permute-start(f32[8,128]{1,0:T(8,128)S(1)} %get-tuple-element.45), channel_id=1, source_target_pairs={{0,4},{1,5},{2,6},{3,7},{4,8},{5,9},{6,10},{7,11},{8,12},{9,13},{1... | collective-permute-start | bytes 12296 | tf_op jit(solution)/shard_map/ppermute | solution.py:258
  65.6 4.9 %compare_far.1 = (f32[8,768]{1,0:T(8,128)}, f32[8,128]{1,0:T(8,128)S(1)}, f32[8,128]{1,0:T(8,128)S(1)}, f32[8,128]{1,0:T(8,128)S(1)}) custom-call(f32[8,768]{1,0:T(8,128)S(1)} %get-tuple-element.39.before_ref, bf16[784,1024]{1,0:T(8,128)(2,1)S(1)} %collective-permute-done.13.refs_0_, bf16[784,1024]{1,0:T(8,128)(2,1)S(1)} %gather.1.refs_0_.refs_1_, ...), custom_call_target="tpu_custom_call" | custom-call | flops 3623878656 | bytes 1572864 | tf_op jit(solution)/shard_map/compare_far/pallas_call | solution.py:218
  71.6 1.6 %collective-permute-start.17 = (f32[8,128]{1,0:T(8,128)S(1)}, f32[8,128]{1,0:T(8,128)S(1)}, u32[]{:S(2)}, u32[]{:S(2)}) collective-permute-start(f32[8,128]{1,0:T(8,128)S(1)} %get-tuple-element.50), channel_id=1, source_target_pairs={{0,8},{1,9},{2,10},{3,11},{4,12},{5,13},{6,14},{7,15},{8,0},{9,1},... | collective-permute-start | bytes 12296 | tf_op jit(solution)/shard_map/ppermute | solution.py:258
  75.6 7.2 %all_to_all.11 = f32[4,2,128]{2,1,0:T(2,128)S(1)} all-to-all(f32[4,2,128]{2,1,0:T(2,128)S(1)} %bitcast.8), channel_id=1, replica_groups={{0,32,64,96},{4,36,68,100},{8,40,72,104},{12,44,76,108},{1,33,65,97},{5..., dimensions={0} | all-to-all | bytes 8192 | tf_op jit(solution)/shard_map/all_to_all | solution.py:278
  82.8 6.6 %collective-permute-start.18 = (f32[8,128]{1,0:T(8,128)S(1)}, f32[8,128]{1,0:T(8,128)S(1)}, u32[]{:S(2)}, u32[]{:S(2)}) collective-permute-start(f32[8,128]{1,0:T(8,128)S(1)} %bitcast.5), channel_id=1, source_target_pairs={{0,16},{1,17},{2,18},{3,19},{4,20},{5,21},{6,22},{7,23},{8,24},{9,... | collective-permute-start | bytes 12296 | tf_op jit(solution)/shard_map/ppermute | solution.py:263
  (31 shorter events, 9.9 us)
Async XLA Ops:
  1.4 1.6 %copy-start = (f32[512,1024]{1,0:T(8,128)S(1)}, f32[512,1024]{1,0:T(8,128)}, u32[]{:S(2)}) copy-start(f32[512,1024]{1,0:T(8,128)} %emb_ref.1) | copy-start | bytes 6291460
  4.7 6.4 %collective-permute-start.3 = (bf16[448,1024]{1,0:T(8,128)(2,1)S(1)}, bf16[448,1024]{1,0:T(8,128)(2,1)S(1)}, u32[]{:S(2)}, u32[]{:S(2)}) collective-permute-start(bf16[448,1024]{1,0:T(8,128)(2,1)S(1)} %get-tuple-element.33), channel_id=1, source_target_pairs={{0,16},{1,17},{2,18},{3,19},{4,20},{5,21},{6,22},{7,23},{8,24},{9,... | collective-permute-start | bytes 2752520 | tf_op jit(solution)/shard_map/ppermute | solution.py:263
  6.2 7.1 %collective-permute-start = (bf16[112,1024]{1,0:T(8,128)(2,1)S(1)}, bf16[112,1024]{1,0:T(8,128)(2,1)S(1)}, u32[]{:S(2)}, u32[]{:S(2)}) collective-permute-start(bf16[112,1024]{1,0:T(8,128)(2,1)S(1)} %get-tuple-element.30), channel_id=1, source_target_pairs={{0,32},{1,33},{2,34},{3,35},{4,36},{5,37},{6,38},{7,39},{8,40},{9,... | collective-permute-start | bytes 688136 | tf_op jit(solution)/shard_map/ppermute | solution.py:271
  7.5 8.6 %collective-permute-start.1 = (bf16[112,1024]{1,0:T(8,128)(2,1)S(1)}, bf16[112,1024]{1,0:T(8,128)(2,1)S(1)}, u32[]{:S(2)}, u32[]{:S(2)}) collective-permute-start(bf16[112,1024]{1,0:T(8,128)(2,1)S(1)} %get-tuple-element.31), channel_id=1, source_target_pairs={{0,64},{1,65},{2,66},{3,67},{4,68},{5,69},{6,70},{7,71},{8,72},{9,... | collective-permute-start | bytes 688136 | tf_op jit(solution)/shard_map/ppermute | solution.py:271
  9.9 6.2 %collective-permute-start.2 = (bf16[112,1024]{1,0:T(8,128)(2,1)S(1)}, bf16[112,1024]{1,0:T(8,128)(2,1)S(1)}, u32[]{:S(2)}, u32[]{:S(2)}) collective-permute-start(bf16[112,1024]{1,0:T(8,128)(2,1)S(1)} %get-tuple-element.32), channel_id=1, source_target_pairs={{0,96},{1,97},{2,98},{3,99},{4,100},{5,101},{6,102},{7,103},{8,104... | collective-permute-start | bytes 688136 | tf_op jit(solution)/shard_map/ppermute | solution.py:271
  11.1 6.9 %collective-permute-start.6 = (bf16[112,1024]{1,0:T(8,128)(2,1)S(1)}, bf16[112,1024]{1,0:T(8,128)(2,1)S(1)}, u32[]{:S(2)}, u32[]{:S(2)}) collective-permute-start(bf16[112,1024]{1,0:T(8,128)(2,1)S(1)} %get-tuple-element.51), channel_id=1, source_target_pairs={{0,96},{1,97},{2,98},{3,99},{4,100},{5,101},{6,102},{7,103},{8,104... | collective-permute-start | bytes 688136 | tf_op jit(solution)/shard_map/ppermute | solution.py:271
  11.2 7.3 %collective-permute-start.5 = (bf16[112,1024]{1,0:T(8,128)(2,1)S(1)}, bf16[112,1024]{1,0:T(8,128)(2,1)S(1)}, u32[]{:S(2)}, u32[]{:S(2)}) collective-permute-start(bf16[112,1024]{1,0:T(8,128)(2,1)S(1)} %get-tuple-element.52), channel_id=1, source_target_pairs={{0,64},{1,65},{2,66},{3,67},{4,68},{5,69},{6,70},{7,71},{8,72},{9,... | collective-permute-start | bytes 688136 | tf_op jit(solution)/shard_map/ppermute | solution.py:271
  13.3 7.7 %collective-permute-start.4 = (bf16[112,1024]{1,0:T(8,128)(2,1)S(1)}, bf16[112,1024]{1,0:T(8,128)(2,1)S(1)}, u32[]{:S(2)}, u32[]{:S(2)}) collective-permute-start(bf16[112,1024]{1,0:T(8,128)(2,1)S(1)} %get-tuple-element.53), channel_id=1, source_target_pairs={{0,32},{1,33},{2,34},{3,35},{4,36},{5,37},{6,38},{7,39},{8,40},{9,... | collective-permute-start | bytes 688136 | tf_op jit(solution)/shard_map/ppermute | solution.py:271
  21.1 21.3 %collective-permute-start.7 = (bf16[784,1024]{1,0:T(8,128)(2,1)S(1)}, bf16[784,1024]{1,0:T(8,128)(2,1)S(1)}, u32[]{:S(2)}, u32[]{:S(2)}) collective-permute-start(bf16[784,1024]{1,0:T(8,128)(2,1)S(1)} %gather.1.refs_0_.refs_1_), channel_id=1, source_target_pairs={{0,12},{1,13},{2,14},{3,15},{4,0},{5,1},{6,2},{7,3},{8,4},{9,5},{1... | collective-permute-start | bytes 4816904 | tf_op jit(solution)/shard_map/ppermute | solution.py:258
  22.5 21.5 %collective-permute-start.8 = (bf16[784,1024]{1,0:T(8,128)(2,1)S(1)}, bf16[784,1024]{1,0:T(8,128)(2,1)S(1)}, u32[]{:S(2)}, u32[]{:S(2)}) collective-permute-start(bf16[784,1024]{1,0:T(8,128)(2,1)S(1)} %gather.1.refs_0_.refs_1_), channel_id=1, source_target_pairs={{0,3},{1,0},{2,1},{3,2},{4,7},{5,4},{6,5},{7,6},{8,11},{9,8},{10,9... | collective-permute-start | bytes 4816904 | tf_op jit(solution)/shard_map/ppermute | solution.py:258
  26.3 21.3 %collective-permute-start.9 = (bf16[784,1024]{1,0:T(8,128)(2,1)S(1)}, bf16[784,1024]{1,0:T(8,128)(2,1)S(1)}, u32[]{:S(2)}, u32[]{:S(2)}) collective-permute-start(bf16[784,1024]{1,0:T(8,128)(2,1)S(1)} %gather.1.refs_0_.refs_1_), channel_id=1, source_target_pairs={{0,1},{1,2},{2,3},{3,0},{4,5},{5,6},{6,7},{7,4},{8,9},{9,10},{10,1... | collective-permute-start | bytes 4816904 | tf_op jit(solution)/shard_map/ppermute | solution.py:258
  42.4 23.2 %collective-permute-start.13 = (bf16[784,1024]{1,0:T(8,128)(2,1)S(1)}, bf16[784,1024]{1,0:T(8,128)(2,1)S(1)}, u32[]{:S(2)}, u32[]{:S(2)}) collective-permute-start(bf16[784,1024]{1,0:T(8,128)(2,1)S(1)} %collective-permute-done.7.refs_2_.refs_3_), channel_id=1, source_target_pairs={{0,12},{1,13},{2,14},{3,15},{4,0},{5,1},{6,2},{7,3},{8,4},{9,5},{1... | collective-permute-start | bytes 4816904 | tf_op jit(solution)/shard_map/ppermute | solution.py:258
  44.0 16.1 %collective-permute-start.11 = (bf16[400,1024]{1,0:T(8,128)(2,1)S(1)}, bf16[400,1024]{1,0:T(8,128)(2,1)S(1)}, u32[]{:S(2)}, u32[]{:S(2)}) collective-permute-start(bf16[400,1024]{1,0:T(8,128)(2,1)S(1)} %slice.28), channel_id=1, source_target_pairs={{0,3},{1,0},{2,1},{3,2},{4,7},{5,4},{6,5},{7,6},{8,11},{9,8},{10,9... | collective-permute-start | bytes 2457608 | tf_op jit(solution)/shard_map/ppermute | solution.py:258
  47.6 12.6 %collective-permute-start.12 = (bf16[384,1024]{1,0:T(8,128)(2,1)S(1)}, bf16[384,1024]{1,0:T(8,128)(2,1)S(1)}, u32[]{:S(2)}, u32[]{:S(2)}) collective-permute-start(bf16[384,1024]{1,0:T(8,128)(2,1)S(1)} %slice.29), channel_id=1, source_target_pairs={{0,1},{1,2},{2,3},{3,0},{4,5},{5,6},{6,7},{7,4},{8,9},{9,10},{10,1... | collective-permute-start | bytes 2359304 | tf_op jit(solution)/shard_map/ppermute | solution.py:258
  54.2 3.5 %collective-permute-start.10 = (f32[8,128]{1,0:T(8,128)S(1)}, f32[8,128]{1,0:T(8,128)S(1)}, u32[]{:S(2)}, u32[]{:S(2)}) collective-permute-start(f32[8,128]{1,0:T(8,128)S(1)} %get-tuple-element.36), channel_id=1, source_target_pairs={{0,3},{1,0},{2,1},{3,2},{4,7},{5,4},{6,5},{7,6},{8,11},{9,8},{10,9... | collective-permute-start | bytes 12296 | tf_op jit(solution)/shard_map/ppermute | solution.py:258
  63.7 6.8 %collective-permute-start.14 = (f32[8,128]{1,0:T(8,128)S(1)}, f32[8,128]{1,0:T(8,128)S(1)}, u32[]{:S(2)}, u32[]{:S(2)}) collective-permute-start(f32[8,128]{1,0:T(8,128)S(1)} %get-tuple-element.44), channel_id=1, source_target_pairs={{0,2},{1,3},{2,0},{3,1},{4,6},{5,7},{6,4},{7,5},{8,10},{9,11},{10,... | collective-permute-start | bytes 12296 | tf_op jit(solution)/shard_map/ppermute | solution.py:258
  63.8 6.7 %collective-permute-start.15 = (f32[8,128]{1,0:T(8,128)S(1)}, f32[8,128]{1,0:T(8,128)S(1)}, u32[]{:S(2)}, u32[]{:S(2)}) collective-permute-start(f32[8,128]{1,0:T(8,128)S(1)} %get-tuple-element.45), channel_id=1, source_target_pairs={{0,4},{1,5},{2,6},{3,7},{4,8},{5,9},{6,10},{7,11},{8,12},{9,13},{1... | collective-permute-start | bytes 12296 | tf_op jit(solution)/shard_map/ppermute | solution.py:258
  70.6 3.7 %collective-permute-start.16 = (f32[8,128]{1,0:T(8,128)S(1)}, f32[8,128]{1,0:T(8,128)S(1)}, u32[]{:S(2)}, u32[]{:S(2)}) collective-permute-start(f32[8,128]{1,0:T(8,128)S(1)} %get-tuple-element.49), channel_id=1, source_target_pairs={{0,1},{1,2},{2,3},{3,0},{4,5},{5,6},{6,7},{7,4},{8,9},{9,10},{10,1... | collective-permute-start | bytes 12296 | tf_op jit(solution)/shard_map/ppermute | solution.py:258
  71.6 4.0 %collective-permute-start.17 = (f32[8,128]{1,0:T(8,128)S(1)}, f32[8,128]{1,0:T(8,128)S(1)}, u32[]{:S(2)}, u32[]{:S(2)}) collective-permute-start(f32[8,128]{1,0:T(8,128)S(1)} %get-tuple-element.50), channel_id=1, source_target_pairs={{0,8},{1,9},{2,10},{3,11},{4,12},{5,13},{6,14},{7,15},{8,0},{9,1},... | collective-permute-start | bytes 12296 | tf_op jit(solution)/shard_map/ppermute | solution.py:258
  82.8 7.4 %collective-permute-start.18 = (f32[8,128]{1,0:T(8,128)S(1)}, f32[8,128]{1,0:T(8,128)S(1)}, u32[]{:S(2)}, u32[]{:S(2)}) collective-permute-start(f32[8,128]{1,0:T(8,128)S(1)} %bitcast.5), channel_id=1, source_target_pairs={{0,16},{1,17},{2,18},{3,19},{4,20},{5,21},{6,22},{7,23},{8,24},{9,... | collective-permute-start | bytes 12296 | tf_op jit(solution)/shard_map/ppermute | solution.py:263
